TPU v7x, 32 devices: a whole 2x2x4 slice. The times are simulated.
32 devices in a mesh: row: 4 (over y, core), col: 8 (over z, x).
Axes of the slice: x: 2, y: 2, z: 4, core: 2. Of those that a mesh axis runs over, the one named last changes fastest.
Arguments:
- points: bfloat16 [262144, 768], P(('row', 'col')), may hold values from -6 to 6
- node_of_row: int32 [262144], P(('row', 'col')), may hold values from 0 to 63, as said below
- init_axes: float32 [768, 8], replicated, may hold values from -0.21875 to 0.21875
Outputs:
- projected: float32 [8, 262144], P(None, ('row', 'col'))
Inputs may be any that keep to these rules, and one draw needn't show every extreme that they name: `node_of_row`: never falls along the points; every one of the 64 nodes has at least 512 points; the points of one device belong to at most 8 nodes, and exactly 8 on some device; a node may cover many devices.
All inputs are finite; a program needn't handle non-finite values.
Results may differ from a plain program's by a relative error of at most 0.0035.
The roundings to bfloat16 on the way count: a program that leaves them out, or rounds other values in their place, can miss the bound.
Values sent between devices are 32-bit elements; how exact they have to be, the bound alone decides.
No kernel may reach another device: no remote copies, remote signals or barrier semaphores. Data moves between devices by JAX's collectives and lax.ppermute only.
A program may use at most 128 MiB of HBM per device.

v0:
```python
import jax
import jax.numpy as jnp
from jax import lax
from jax.sharding import PartitionSpec as P

AXES = 8
ITERS = 3
SPAN_MOST = 8


def orthonormal(moment):
    found = []
    for index in range(moment.shape[1]):
        vector = moment[:, index]
        for column in found:
            vector = vector - jnp.sum(column * vector) * column
        vector = vector / jnp.sqrt(jnp.sum(vector * vector))
        found.append(vector)
    return jnp.stack(found, 1)


def lifted_terms(block, frames, centre):
    offset = jnp.einsum("ld,ldk->lk", centre, frames, precision=lax.Precision.HIGHEST)
    flat_frames = frames.astype(jnp.bfloat16).transpose(1, 0, 2).reshape(frames.shape[1], -1)
    spread = jnp.dot(block, flat_frames, preferred_element_type=jnp.float32)
    return spread.reshape(block.shape[0], SPAN_MOST, AXES) - offset[None]


def local_moment(block, member, frames, centre):
    terms = lifted_terms(block, frames, centre)
    lifted = terms.astype(jnp.bfloat16) * member.astype(jnp.bfloat16)[:, :, None]
    moment = lax.dot_general(
        block,
        lifted.reshape(block.shape[0], -1),
        (((0,), (0,)), ((), ())),
        preferred_element_type=jnp.float32,
    )
    moment = moment.reshape(block.shape[1], SPAN_MOST, AXES).transpose(1, 0, 2)
    column_sums = jnp.sum(lifted.astype(jnp.float32), 0)
    return moment - centre[:, :, None] * column_sums[:, None, :]


def settle(pieces, first_node, last_node):
    span_count = last_node - first_node
    first_mark = first_node.astype(jnp.float32)
    last_mark = last_node.astype(jnp.float32)
    flat_parts = [piece.reshape(piece.shape[0], -1) for piece in pieces]
    head_rows = tuple((flat[0:1] for flat in flat_parts))
    tail_rows = tuple((lax.dynamic_slice_in_dim(flat, span_count, 1, 0) for flat in flat_parts))
    tail_only = tuple((jnp.where(span_count > 0, tail, 0.0) for tail in tail_rows))
    node_marks = jnp.stack([first_mark, last_mark]).reshape(1, 2)
    gathered = lax.all_gather(
        (node_marks,) + head_rows + tail_only, ("row", "col"), axis=0, tiled=True
    )
    marks_all = gathered[0]
    count_parts = len(flat_parts)
    not_self = jnp.arange(marks_all.shape[0], dtype=jnp.int32) != lax.axis_index(("row", "col"))
    head_first = (not_self & (marks_all[:, 0] == first_mark))[:, None]
    tail_first = (not_self & (marks_all[:, 1] == first_mark))[:, None]
    head_last = (not_self & (marks_all[:, 0] == last_mark) & (last_node != first_node))[:, None]
    tail_last = (not_self & (marks_all[:, 1] == last_mark) & (last_node != first_node))[:, None]
    into_first = []
    into_last = []
    for index in range(count_parts):
        heads_all = gathered[1 + index]
        tails_all = gathered[1 + count_parts + index]
        into_first.append(
            jnp.sum(
                jnp.where(head_first, heads_all, 0.0) + jnp.where(tail_first, tails_all, 0.0),
                0,
                keepdims=True,
            )
        )
        into_last.append(
            jnp.sum(
                jnp.where(head_last, heads_all, 0.0) + jnp.where(tail_last, tails_all, 0.0),
                0,
                keepdims=True,
            )
        )
    slot_index = jnp.arange(SPAN_MOST, dtype=jnp.int32)[:, None]
    settled = []
    for piece, flat, add_first, add_last in zip(pieces, flat_parts, into_first, into_last):
        whole = (
            flat
            + jnp.where(slot_index == 0, add_first, 0.0)
            + jnp.where(slot_index == span_count, add_last, 0.0)
        )
        settled.append(whole.reshape(piece.shape))
    return settled


def shards(points, node_of_row, init_axes):
    row_count = points.shape[0]
    width = points.shape[1]
    first_node = node_of_row[0]
    last_node = node_of_row[-1]
    slot_index = jnp.arange(SPAN_MOST, dtype=jnp.int32)
    member = (node_of_row[:, None] - first_node == slot_index[None, :]).astype(jnp.float32)
    node_sums = lax.dot_general(
        member.astype(jnp.bfloat16),
        points,
        (((0,), (0,)), ((), ())),
        preferred_element_type=jnp.float32,
    )
    node_counts = jnp.sum(member, 0)
    node_sums, node_counts = settle([node_sums, node_counts], first_node, last_node)
    live_slot = slot_index <= last_node - first_node
    centre = node_sums / jnp.where(live_slot, node_counts, 1.0)[:, None]
    start_frames = jnp.broadcast_to(init_axes, (SPAN_MOST, width, AXES))
    frames = start_frames
    for repeat in range(ITERS):
        moment = local_moment(points, member, frames, centre)
        (moment,) = settle([moment], first_node, last_node)
        moment = jnp.where(live_slot[:, None, None], moment, start_frames)
        frames = jax.vmap(orthonormal)(moment)
    terms = lifted_terms(points, frames, centre)
    coords = jnp.sum(terms * member[:, :, None], 1)
    return coords.reshape(row_count, AXES).T


def solution(mesh):
    in_specs = (P(("row", "col"), None), P(("row", "col")), P())
    out_specs = P(None, ("row", "col"))
    return jax.shard_map(shards, mesh=mesh, in_specs=in_specs, out_specs=out_specs, check_vma=False)
```

profile of v0, /device:TPU:0, one launch (start us, length us, event | category | flops | bytes accessed | tf_op | source)
XLA Modules:
  0.0 698.4 jit_solution(12650673568220418087)
XLA Ops:
  0.0 1.3 fusion.100
  1.3 1.4 broadcast_subtract_fusion
  2.7 0.7 fusion.35
  7.6 0.6 slice_dynamic-update-slice_fusion
  8.9 42.1 %all-reduce.3 = (f32[64]{0:T(128)S(1)}, f32[32]{0:T(128)S(1)}, f32[32]{0:T(128)S(1)}) all-reduce(f32[64]{0:T(128)S(1)} %maximum_dynamic-update-slice_fusion, f32[32]{0:T(128)S(1)} %bitcast_dynamic-update-slice_fusion, f32[32]{0:T(128)S(1)} %get-tuple-element.200), channel_id=2, replica_groups=mesh['row'=4,'col'=8] {'row','col'}, use_global_device_ids=true, to_apply=%add | all-reduce | flops 128 | bytes 1024
  51.5 0.7 add_reduce_fusion.1
  52.2 1.8 add_select_fusion.3
  54.0 6.6 fusion.83
  60.6 66.3 %all-gather.3 = f32[32,1,768]{2,1,0:T(1,128)S(1)} all-gather(f32[1,1,768]{2,1,0:T(1,128)S(1)} %get-tuple-element.193), channel_id=1, replica_groups=mesh['row'=4,'col'=8] {'row','col'}, dimensions={0}, use_global_device_ids=true | all-gather | bytes 101376 | tf_op jit(solution)/shard_map/all_gather | solution.py:52
  126.9 63.8 %all-gather.2 = f32[32,1,768]{2,1,0:T(1,128)S(1)} all-gather(f32[1,1,768]{2,1,0:T(1,128)S(1)} %get-tuple-element.192), channel_id=1, replica_groups=mesh['row'=4,'col'=8] {'row','col'}, dimensions={0}, use_global_device_ids=true | all-gather | bytes 101376 | tf_op jit(solution)/shard_map/all_gather | solution.py:52
  191.1 0.4 fusion.53
  191.5 4.0 convert_reduce_fusion.2
  195.5 2.3 convolution_bitcast_fusion.3
  197.9 0.8 bitcast_subtract_fusion.2
  198.7 1.9 copy.198
  200.6 2.8 reshape.2393
  203.4 1.0 fusion.56
  204.3 69.8 %all-gather.5 = f32[32,1,6144]{2,1,0:T(1,128)S(1)} all-gather(f32[1,1,6144]{2,1,0:T(1,128)S(1)} %fusion.56), channel_id=1, replica_groups=mesh['row'=4,'col'=8] {'row','col'}, dimensions={0}, use_global_device_ids=true | all-gather | bytes 811008 | tf_op jit(solution)/shard_map/all_gather | solution.py:52
  274.1 0.9 slice.165
  275.4 68.4 %all-gather.4 = f32[32,1,6144]{2,1,0:T(1,128)S(1)} all-gather(f32[1,1,6144]{2,1,0:T(1,128)S(1)} %reshape.2414), channel_id=1, replica_groups=mesh['row'=4,'col'=8] {'row','col'}, dimensions={0}, use_global_device_ids=true | all-gather | bytes 811008 | tf_op jit(solution)/shard_map/all_gather | solution.py:52
  343.8 1.5 fusion.30
  346.1 0.9 add_select_fusion.2
  347.3 0.3 fusion.75
  351.1 0.5 fusion.40
  351.7 8.6 %convert_reduce_fusion.1 = (f32[64]{0:T(128)S(1)}, bf16[8192,64]{0,1:T(8,128)(2,1)S(1)}) fusion(bf16[8192,8]{0,1:T(8,128)(2,1)S(1)} %get-tuple-element.188, f32[64]{0:T(128)S(1)} %sub.799, bf16[8192,768]{1,0:T(8,128)(2,1)} %param.3, bf16[768,8,8]{0,1,2:T(8,128)(2,1)S(1)} %convert_bitcast_fusion.2), kind=kOutput, calls=%fused_computation.17 | convolution fusion | flops 807927744 | bytes 13861376 | tf_op jit(solution)/shard_map/dot_general | solution.py:25
  360.3 6.9 convolution_bitcast_fusion.2
  367.3 0.8 bitcast_subtract_fusion.1
  368.1 1.9 copy.205
  370.0 2.8 reshape.2396
  372.7 1.0 fusion.57
  373.7 69.5 %all-gather.7 = f32[32,1,6144]{2,1,0:T(1,128)S(1)} all-gather(f32[1,1,6144]{2,1,0:T(1,128)S(1)} %fusion.57), channel_id=1, replica_groups=mesh['row'=4,'col'=8] {'row','col'}, dimensions={0}, use_global_device_ids=true | all-gather | bytes 811008 | tf_op jit(solution)/shard_map/all_gather | solution.py:52
  443.2 0.9 slice.174
  444.5 68.6 %all-gather.6 = f32[32,1,6144]{2,1,0:T(1,128)S(1)} all-gather(f32[1,1,6144]{2,1,0:T(1,128)S(1)} %reshape.2418), channel_id=1, replica_groups=mesh['row'=4,'col'=8] {'row','col'}, dimensions={0}, use_global_device_ids=true | all-gather | bytes 811008 | tf_op jit(solution)/shard_map/all_gather | solution.py:52
  513.1 1.5 fusion.26
  515.3 0.9 add_select_fusion.1
  520.4 0.5 fusion.38
  521.0 8.6 %convert_reduce_fusion = (f32[64]{0:T(128)S(1)}, bf16[8192,64]{0,1:T(8,128)(2,1)S(1)}) fusion(bf16[8192,8]{0,1:T(8,128)(2,1)S(1)} %get-tuple-element.188, f32[64]{0:T(128)S(1)} %sub.859, bf16[8192,768]{1,0:T(8,128)(2,1)} %param.3, bf16[768,8,8]{0,1,2:T(8,128)(2,1)S(1)} %convert_bitcast_fusion.1), kind=kOutput, calls=%fused_computation.16 | convolution fusion | flops 807927744 | bytes 13861376 | tf_op jit(solution)/shard_map/dot_general | solution.py:25
  529.6 6.9 convolution_bitcast_fusion.1
  536.6 0.8 bitcast_subtract_fusion
  537.4 1.9 copy.212
  539.3 2.8 reshape.2399
  542.1 1.0 fusion.58
  543.0 69.7 %all-gather.9 = f32[32,1,6144]{2,1,0:T(1,128)S(1)} all-gather(f32[1,1,6144]{2,1,0:T(1,128)S(1)} %fusion.58), channel_id=1, replica_groups=mesh['row'=4,'col'=8] {'row','col'}, dimensions={0}, use_global_device_ids=true | all-gather | bytes 811008 | tf_op jit(solution)/shard_map/all_gather | solution.py:52
  612.8 0.9 slice.183
  614.1 68.2 %all-gather.8 = f32[32,1,6144]{2,1,0:T(1,128)S(1)} all-gather(f32[1,1,6144]{2,1,0:T(1,128)S(1)} %reshape.2422), channel_id=1, replica_groups=mesh['row'=4,'col'=8] {'row','col'}, dimensions={0}, use_global_device_ids=true | all-gather | bytes 811008 | tf_op jit(solution)/shard_map/all_gather | solution.py:52
  682.3 0.8 fusion.22
  688.2 0.5 fusion.36
  688.8 9.2 %fusion.19 = f32[8192,8]{0,1:T(8,128)} fusion(bf16[8192,768]{1,0:T(8,128)(2,1)} %param.3, f32[8192,8]{0,1:T(8,128)} %get-tuple-element.189, f32[8,8]{1,0:T(8,128)S(1)} %bitcast.467, bf16[768,8,8]{0,1,2:T(8,128)(2,1)S(1)} %convert_bitcast_fusion), kind=kOutput, calls=%fused_computation.19 | convolution fusion | flops 806813696 | bytes 13205760 | tf_op jit(solution)/shard_map/dot_general | solution.py:25
  (168 shorter events, 17.3 us)
Async XLA Ops:
  0.0 191.0 %copy-start.1 = (f32[768,8]{0,1:T(8,128)S(1)}, f32[768,8]{0,1:T(8,128)}, u32[]{:S(2)}) copy-start(f32[768,8]{0,1:T(8,128)} %param.5) | copy-start | bytes 73732
  51.3 139.6 %copy-start.2 = (pred[32]{0:T(512)(128)(4,1)}, pred[32]{0:T(512)(128)(4,1)S(1)}, u32[]{:S(2)}) copy-start(pred[32]{0:T(512)(128)(4,1)S(1)} %get-tuple-element.194) | copy-start | bytes 100
  51.3 139.6 %copy-start.4 = (pred[32]{0:T(512)(128)(4,1)}, pred[32]{0:T(512)(128)(4,1)S(1)}, u32[]{:S(2)}) copy-start(pred[32]{0:T(512)(128)(4,1)S(1)} %get-tuple-element.196) | copy-start | bytes 100
  51.3 139.6 %copy-start.6 = (pred[32]{0:T(512)(128)(4,1)}, pred[32]{0:T(512)(128)(4,1)S(1)}, u32[]{:S(2)}) copy-start(pred[32]{0:T(512)(128)(4,1)S(1)} %get-tuple-element.198) | copy-start | bytes 100
  51.5 140.0 %copy-start = (bf16[8192,768]{1,0:T(8,128)(2,1)S(1)}, bf16[8192,768]{1,0:T(8,128)(2,1)}, u32[]{:S(2)}) copy-start(bf16[8192,768]{1,0:T(8,128)(2,1)} %param.3) | copy-start | bytes 37748740
  190.9 7.0 %copy-start.8 = (pred[8]{0:T(512)(128)(4,1)}, pred[8]{0:T(512)(128)(4,1)S(1)}, u32[]{:S(2)}) copy-start(pred[8]{0:T(512)(128)(4,1)S(1)} %iota_compare_fusion.2) | copy-start | bytes 28
  190.9 6.9 copy-start.10
  346.0 1.9 copy-start.12
  529.5 152.8 %copy-start.3 = (pred[32]{0:T(512)(128)(4,1)S(1)}, pred[32]{0:T(512)(128)(4,1)}, u32[]{:S(2)}) copy-start(pred[32]{0:T(512)(128)(4,1)} %copy-done.2) | copy-start | bytes 100
  529.6 152.8 %copy-start.5 = (pred[32]{0:T(512)(128)(4,1)S(1)}, pred[32]{0:T(512)(128)(4,1)}, u32[]{:S(2)}) copy-start(pred[32]{0:T(512)(128)(4,1)} %copy-done.4) | copy-start | bytes 100
  529.6 152.8 %copy-start.7 = (pred[32]{0:T(512)(128)(4,1)S(1)}, pred[32]{0:T(512)(128)(4,1)}, u32[]{:S(2)}) copy-start(pred[32]{0:T(512)(128)(4,1)} %copy-done.6) | copy-start | bytes 100
  529.6 154.3 %copy-start.9 = (pred[8]{0:T(512)(128)(4,1)S(1)}, pred[8]{0:T(512)(128)(4,1)}, u32[]{:S(2)}) copy-start(pred[8]{0:T(512)(128)(4,1)} %copy-done.8) | copy-start | bytes 28
  529.6 154.3 %copy-start.11 = (pred[8]{0:T(512)(128)(4,1)S(1)}, pred[8]{0:T(512)(128)(4,1)}, u32[]{:S(2)}) copy-start(pred[8]{0:T(512)(128)(4,1)} %copy-done.10) | copy-start | bytes 28
  529.6 154.3 %copy-start.13 = (pred[8]{0:T(512)(128)(4,1)S(1)}, pred[8]{0:T(512)(128)(4,1)}, u32[]{:S(2)}) copy-start(pred[8]{0:T(512)(128)(4,1)} %copy-done.12) | copy-start | bytes 28
where the time goes:
time: 707 us; the launch traced here: 698 us
  blocking collectives  586 us (83%)
  matrix products  54.8 us (8%)
  other arithmetic  28.4 us (4%)
  local copies, waits for them, and re-layouts  23.1 us (3%)
    all_gather x8, blocking collectives, settle(): lax.all_gather((node_marks,) + head_rows + tail_only, ('row', 'col'), axi...  544 us
    unnamed x1, blocking collectives  42.1 us
    dot_general x4, matrix products, lifted_terms(): spread = jnp.dot(block, flat_frames, preferred_element_type=jnp.float32)  30.3 us
    dot_general x3, matrix products, local_moment(): lax.dot_general(block, lifted.reshape(block.shape[0], -1), (((0,), (0,)),...  16 us

commit v1 on v0

v1 whole, which is shorter than its diff:
```python
import functools

import jax
import jax.numpy as jnp
from jax import lax
from jax.experimental import pallas as pl
from jax.experimental.pallas import tpu as pltpu
from jax.sharding import PartitionSpec as P

ITERS = 3
SLOTS = 8
LANES = 128
BLOCK = 1024
F32 = jnp.float32
BF16 = jnp.bfloat16
MIB = 1 << 20


def dot_nt(a, b):
    return lax.dot_general(a, b, (((1,), (1,)), ((), ())), preferred_element_type=F32)


def dot_nn(a, b):
    return lax.dot_general(a, b, (((1,), (0,)), ((), ())), preferred_element_type=F32)


def fold_lanes(value):
    total = value[:, :LANES]
    for start in range(LANES, value.shape[1], LANES):
        total = total + value[:, start : start + LANES]
    return total


def same(a, b):
    return jnp.where(a == b, 1.0, 0.0).astype(F32)


def put_rows(tall_ref, value, at, flat):
    size = value.shape[0]
    for tile in range(value.shape[1] // LANES):
        tall_ref[pl.ds(tile * flat + at, size), :] = value[:, tile * LANES : (tile + 1) * LANES]


def put_strided(tall_ref, value, index, axes):
    flat = SLOTS * axes
    for tile in range(value.shape[1] // LANES):
        tall_ref[pl.ds(tile * flat + index, SLOTS, stride=axes), :] = value[
            :, tile * LANES : (tile + 1) * LANES
        ]


def get_strided(tall_ref, index, axes):
    flat = SLOTS * axes
    tiles = tall_ref.shape[0] // flat
    return jnp.concatenate(
        [tall_ref[pl.ds(tile * flat + index, SLOTS, stride=axes), :] for tile in range(tiles)], 1
    )


def get_flat(tall_ref, flat):
    tiles = tall_ref.shape[0] // flat
    return jnp.concatenate([tall_ref[tile * flat : (tile + 1) * flat, :] for tile in range(tiles)], 1)


def ends_of(nodes_ref):
    nodes = nodes_ref[...]
    return jnp.min(nodes), jnp.max(nodes)


def first_sweep_kernel(axes, points_ref, nodes_ref, init_ref, part_ref, sums_ref, note_ref):
    rows, width = points_ref.shape
    first, last = ends_of(nodes_ref)
    frame = init_ref[...].T.astype(BF16)
    slot_rows = SLOTS * axes
    moment = jnp.zeros((2 * slot_rows + SLOTS, width), F32)
    columns = jnp.zeros((slot_rows, LANES), F32)
    counts = jnp.zeros((SLOTS, LANES), F32)
    for start in range(0, rows, BLOCK):
        block = points_ref[start : start + BLOCK, :]
        slot_of = nodes_ref[:, start : start + BLOCK] - first
        spread = dot_nt(frame, block)
        high = spread.astype(BF16).astype(F32)
        low = (spread - high).astype(BF16).astype(F32)
        highs = []
        lows = []
        for slot in range(SLOTS):
            here = slot_of == slot
            highs.append(jnp.where(here, high, 0.0))
            lows.append(jnp.where(here, low, 0.0))
        highs = jnp.concatenate(highs, 0)
        lows = jnp.concatenate(lows, 0)
        member = (slot_of == lax.broadcasted_iota(jnp.int32, (SLOTS, BLOCK), 0)).astype(F32)
        left = jnp.concatenate([highs.astype(BF16), lows.astype(BF16), member.astype(BF16)], 0)
        moment = moment + dot_nn(left, block)
        columns = columns + fold_lanes(highs + lows)
        counts = counts + fold_lanes(member)
    part_ref[:, :width] = moment[:slot_rows] + moment[slot_rows : 2 * slot_rows]
    part_ref[:, width:] = jnp.broadcast_to(jnp.sum(columns, 1, keepdims=True), columns.shape)
    sums_ref[:, :width] = moment[2 * slot_rows :]
    sums_ref[:, width:] = jnp.broadcast_to(jnp.sum(counts, 1, keepdims=True), counts.shape)
    span = last - first
    tail = pl.multiple_of(span * axes, axes)
    note_ref[:axes, :] = part_ref[:axes, :]
    note_ref[axes : 2 * axes, :] = part_ref[pl.ds(tail, axes), :]
    base = 2 * axes
    wide = sums_ref.shape[1]
    note_ref[base : base + 1, :] = sums_ref[0:1, :]
    note_ref[base + 1 : base + 2, :] = sums_ref[pl.ds(span, 1), :]
    note_ref[base + 2 : base + 3, :] = jnp.full((1, wide), first.astype(F32))
    note_ref[base + 3 : base + 4, :] = jnp.full((1, wide), last.astype(F32))
    note_ref[base + 4 :, :] = jnp.zeros((4, wide), F32)


def weigh(axes, own, groups):
    base = 2 * axes
    first = own[base + 2 : base + 3, :1]
    last = own[base + 3 : base + 4, :1]
    heads = [g[base + 2 : base + 3, :1] for g in groups]
    tails = [g[base + 3 : base + 4, :1] for g in groups]
    lowest = functools.reduce(jnp.minimum, heads)
    highest = functools.reduce(jnp.maximum, tails)
    weights = []
    for index, (head, tail) in enumerate(zip(heads, tails)):
        other = 0.0 if index == 0 else 1.0
        weights.append(
            (
                same(head, lowest),
                same(tail, highest),
                other * same(head, first) * (1.0 - same(tail, first)),
                other * same(tail, first),
                other * same(head, last),
                other * same(tail, last) * (1.0 - same(head, last)),
            )
        )
    return weights, lowest, highest


def store_weights(weight_ref, weights):
    flat = [w for source in weights for w in source]
    weight_ref[...] = jnp.zeros(weight_ref.shape, F32)
    for index, weight in enumerate(flat):
        weight_ref[index : index + 1, :] = jnp.broadcast_to(weight, (1, LANES))


def load_weights(weight_ref, count):
    flat = [weight_ref[index : index + 1, :1] for index in range(6 * count)]
    return [tuple(flat[6 * k : 6 * k + 6]) for k in range(count)]


def join_own(own_head, own_tail, pairs, weights):
    head, tail = own_head, own_tail
    for (group_head, group_tail), w in zip(pairs[1:], weights[1:]):
        head = head + w[2] * group_head + w[3] * group_tail
        tail = tail + w[4] * group_head + w[5] * group_tail
    return head, tail


def join_group(pairs, weights):
    head = sum(w[0] * pair[0] for pair, w in zip(pairs, weights))
    tail = sum(w[1] * pair[1] for pair, w in zip(pairs, weights))
    return head, tail


def pairs_of(axes, notes):
    return [(note[:axes, :], note[axes : 2 * axes, :]) for note in notes]


def sum_pairs_of(axes, notes):
    base = 2 * axes
    return [(note[base : base + 1, :], note[base + 1 : base + 2, :]) for note in notes]


def first_join_kernel(axes, count, own_ref, *refs):
    groups = refs[:count]
    own_out, group_out, weight_ref = refs[count:]
    weights, lowest, highest = weigh(axes, own_ref, groups)
    store_weights(weight_ref, weights)
    base = 2 * axes
    wide = own_ref.shape[1]
    own_out[base:, :] = own_ref[base:, :]
    group_out[base:, :] = jnp.zeros((8, wide), F32)
    group_out[base + 2 : base + 3, :] = jnp.broadcast_to(lowest, (1, wide))
    group_out[base + 3 : base + 4, :] = jnp.broadcast_to(highest, (1, wide))
    for pairs, at, size in (
        (pairs_of(axes, groups), 0, axes),
        (sum_pairs_of(axes, groups), base, 1),
    ):
        head, tail = join_own(
            own_ref[at : at + size, :], own_ref[at + size : at + 2 * size, :], pairs, weights
        )
        own_out[at : at + size, :] = head
        own_out[at + size : at + 2 * size, :] = tail
        head, tail = join_group(pairs, weights)
        group_out[at : at + size, :] = head
        group_out[at + size : at + 2 * size, :] = tail


def join_kernel(axes, count, own_ref, weight_ref, *refs):
    groups = refs[:count]
    own_out, group_out = refs[count:]
    weights = load_weights(weight_ref, count)
    pairs = pairs_of(axes, groups)
    head, tail = join_own(own_ref[:axes, :], own_ref[axes:, :], pairs, weights)
    own_out[:axes, :] = head
    own_out[axes:, :] = tail
    head, tail = join_group(pairs, weights)
    group_out[:axes, :] = head
    group_out[axes:, :] = tail


def find_frames(axes, columns, centre, live, flat_ref, offset_ref):
    found = list(columns)
    for index in range(axes):
        lead = found[index]
        length = jnp.sum(lead * lead, 1, keepdims=True)
        length = jnp.where(live, length, 1.0)
        for later in range(index + 1, axes):
            share = jnp.sum(lead * found[later], 1, keepdims=True) / length
            found[later] = found[later] - share * lead
        unit = lead / jnp.sqrt(length)
        put_strided(flat_ref, unit, index, axes)
        offset = jnp.sum(centre * unit, 1, keepdims=True)
        put_strided(offset_ref, jnp.broadcast_to(offset, (SLOTS, LANES)), index, axes)


def sweep_blocks(axes, points_ref, nodes_ref, first, flat_ref, offset_ref):
    rows, width = points_ref.shape
    frames = get_flat(flat_ref, SLOTS * axes).astype(BF16)
    offset = offset_ref[:, :1]
    moment = jnp.zeros((SLOTS * axes, width), F32)
    columns = jnp.zeros((SLOTS * axes, LANES), F32)
    for start in range(0, rows, BLOCK):
        block = points_ref[start : start + BLOCK, :]
        slot_of = nodes_ref[:, start : start + BLOCK] - first
        terms = dot_nt(frames, block) - offset
        kept = [
            jnp.where(slot_of == slot, terms[slot * axes : (slot + 1) * axes], 0.0)
            for slot in range(SLOTS)
        ]
        lifted = jnp.concatenate(kept, 0).astype(BF16)
        moment = moment + dot_nn(lifted, block)
        columns = columns + fold_lanes(lifted.astype(F32))
    return moment, jnp.sum(columns, 1, keepdims=True)


def project_blocks(axes, points_ref, nodes_ref, first, flat_ref, offset_ref, out_ref):
    rows = points_ref.shape[0]
    frames = get_flat(flat_ref, SLOTS * axes).astype(BF16)
    offset = offset_ref[:, :1]
    for start in range(0, rows, BLOCK):
        block = points_ref[start : start + BLOCK, :]
        slot_of = nodes_ref[:, start : start + BLOCK] - first
        terms = dot_nt(frames, block) - offset
        out_ref[:, start : start + BLOCK] = sum(
            jnp.where(slot_of == slot, terms[slot * axes : (slot + 1) * axes], 0.0)
            for slot in range(SLOTS)
        )


def emit_part(axes, moment, column_sums, centre, span, part_ref, note_ref):
    for slot in range(SLOTS):
        at = slice(slot * axes, (slot + 1) * axes)
        part_ref[at, :] = moment[at] - column_sums[at] * centre[slot : slot + 1, :]
    tail = pl.multiple_of(span * axes, axes)
    note_ref[:axes, :] = part_ref[:axes, :]
    note_ref[axes:, :] = part_ref[pl.ds(tail, axes), :]


def live_slots(span):
    return lax.broadcasted_iota(jnp.int32, (SLOTS, 1), 0) <= span


def second_sweep_kernel(axes, count, points_ref, nodes_ref, part_ref, sums_ref, own_ref, *refs):
    groups = refs[:count]
    part_out, note_out, centre_ref, weight_ref, flat_ref, offset_ref, whole_ref, total_ref = refs[count:]
    width = points_ref.shape[1]
    first, last = ends_of(nodes_ref)
    span = last - first
    weights, _, _ = weigh(axes, own_ref, groups)
    store_weights(weight_ref, weights)
    base = 2 * axes
    head, tail = join_own(
        own_ref[:axes, :], own_ref[axes:base, :], pairs_of(axes, groups), weights
    )
    flat = SLOTS * axes
    put_rows(whole_ref, part_ref[...], 0, flat)
    put_rows(whole_ref, tail, pl.multiple_of(span * axes, axes), flat)
    put_rows(whole_ref, head, 0, flat)
    head, tail = join_own(
        own_ref[base : base + 1, :], own_ref[base + 1 : base + 2, :], sum_pairs_of(axes, groups), weights
    )
    total_ref[...] = sums_ref[...]
    total_ref[pl.ds(span, 1), :] = tail
    total_ref[:1, :] = head
    live = live_slots(span)
    counts = jnp.where(live, total_ref[:, width : width + 1], 1.0)
    centre = total_ref[:, :width] / counts
    centre_ref[...] = centre
    columns = []
    for index in range(axes):
        column = get_strided(whole_ref, index, axes)
        columns.append(column[:, :width] - column[:, width : width + 1] * centre)
    find_frames(axes, columns, centre, live, flat_ref, offset_ref)
    moment, column_sums = sweep_blocks(axes, points_ref, nodes_ref, first, flat_ref, offset_ref)
    emit_part(axes, moment, column_sums, centre_ref[...], span, part_out, note_out)


def settle_frames(axes, nodes_ref, part_ref, centre_ref, own_ref, weight_ref, groups, flat_ref, offset_ref, whole_ref):
    first, last = ends_of(nodes_ref)
    span = last - first
    weights = load_weights(weight_ref, len(groups))
    head, tail = join_own(own_ref[:axes, :], own_ref[axes:, :], pairs_of(axes, groups), weights)
    flat = SLOTS * axes
    put_rows(whole_ref, part_ref[...], 0, flat)
    put_rows(whole_ref, tail, pl.multiple_of(span * axes, axes), flat)
    put_rows(whole_ref, head, 0, flat)
    columns = [get_strided(whole_ref, index, axes) for index in range(axes)]
    find_frames(axes, columns, centre_ref[...], live_slots(span), flat_ref, offset_ref)
    return first, span


def sweep_kernel(axes, count, points_ref, nodes_ref, part_ref, centre_ref, own_ref, weight_ref, *refs):
    groups = refs[:count]
    part_out, note_out, flat_ref, offset_ref, whole_ref = refs[count:]
    first, span = settle_frames(
        axes, nodes_ref, part_ref, centre_ref, own_ref, weight_ref, groups, flat_ref, offset_ref, whole_ref
    )
    moment, column_sums = sweep_blocks(axes, points_ref, nodes_ref, first, flat_ref, offset_ref)
    emit_part(axes, moment, column_sums, centre_ref[...], span, part_out, note_out)


def project_kernel(axes, count, points_ref, nodes_ref, part_ref, centre_ref, own_ref, weight_ref, *refs):
    groups = refs[:count]
    out_ref, flat_ref, offset_ref, whole_ref = refs[count:]
    first, _ = settle_frames(
        axes, nodes_ref, part_ref, centre_ref, own_ref, weight_ref, groups, flat_ref, offset_ref, whole_ref
    )
    project_blocks(axes, points_ref, nodes_ref, first, flat_ref, offset_ref, out_ref)


def radices(size):
    found = []
    while size % 4 == 0:
        found.append(4)
        size //= 4
    factor = 2
    while size > 1:
        while size % factor == 0:
            found.insert(0, factor)
            size //= factor
        factor += 1
    return found


def stages_of(mesh):
    stages = []
    stride = 1
    for name in ("col", "row"):
        for radix in radices(mesh.shape[name]):
            stages.append((stride, radix))
            stride *= radix
    return stages


def swap(value, stage, devices):
    stride, radix = stage
    groups = [value]
    for shift in range(1, radix):
        pairs = []
        for source in range(devices):
            place = source // stride % radix
            target = source + ((place + shift) % radix - place) * stride
            pairs.append((source, target))
        groups.append(lax.ppermute(value, ("row", "col"), pairs))
    return groups


def shape(*dims):
    return jax.ShapeDtypeStruct(dims, F32)


def call(kernel, outs, scratch=(), limit=8):
    vmem = pl.BlockSpec(memory_space=pltpu.VMEM)

    def run(*args):
        return pl.pallas_call(
            kernel,
            out_shape=outs,
            in_specs=[vmem] * len(args),
            out_specs=jax.tree.map(lambda _: vmem, outs),
            scratch_shapes=scratch,
            compiler_params=pltpu.CompilerParams(vmem_limit_bytes=limit * MIB),
        )(*args)

    return run


def solution(mesh):
    stages = stages_of(mesh)
    devices = mesh.shape["row"] * mesh.shape["col"]

    def shards(points, node_of_row, init_axes):
        rows, width = points.shape
        axes = init_axes.shape[1]
        flat = SLOTS * axes
        wide = width + LANES
        nodes = node_of_row.reshape(1, rows)
        note_rows = 2 * axes + 8
        tall = flat * width // LANES
        frame_scratch = [pltpu.VMEM((tall, LANES), F32), pltpu.VMEM((flat, LANES), F32)]
        part, sums, note = call(
            functools.partial(first_sweep_kernel, axes),
            (shape(flat, wide), shape(SLOTS, wide), shape(note_rows, wide)),
            limit=32,
        )(points, nodes, init_axes)
        own = group = note
        kept = []
        for stage in stages[:-1]:
            groups = swap(group, stage, devices)
            count = len(groups)
            own, group, weight = call(
                functools.partial(first_join_kernel, axes, count),
                (shape(note_rows, wide), shape(note_rows, wide), shape(8 * count, LANES)),
            )(own, *groups)
            kept.append(weight)
        groups = swap(group, stages[-1], devices)
        count = len(groups)
        part, note, centre, weight = call(
            functools.partial(second_sweep_kernel, axes, count),
            (shape(flat, width), shape(2 * axes, width), shape(SLOTS, width), shape(8 * count, LANES)),
            frame_scratch + [pltpu.VMEM((tall + flat, LANES), F32), pltpu.VMEM((SLOTS, wide), F32)],
            limit=32,
        )(points, nodes, part, sums, own, *groups)
        kept.append(weight)
        for repeat in range(1, ITERS):
            own = group = note
            for stage, weight in zip(stages[:-1], kept):
                groups = swap(group, stage, devices)
                own, group = call(
                    functools.partial(join_kernel, axes, len(groups)),
                    (shape(2 * axes, width), shape(2 * axes, width)),
                )(own, weight, *groups)
            groups = swap(group, stages[-1], devices)
            if repeat < ITERS - 1:
                part, note = call(
                    functools.partial(sweep_kernel, axes, len(groups)),
                    (shape(flat, width), shape(2 * axes, width)),
                    frame_scratch + [pltpu.VMEM((tall, LANES), F32)],
                    limit=32,
                )(points, nodes, part, centre, own, kept[-1], *groups)
        return call(
            functools.partial(project_kernel, axes, len(groups)),
            shape(axes, rows),
            frame_scratch + [pltpu.VMEM((tall, LANES), F32)],
            limit=32,
        )(points, nodes, part, centre, own, kept[-1], *groups)

    in_specs = (P(("row", "col"), None), P(("row", "col")), P())
    out_specs = P(None, ("row", "col"))
    return jax.shard_map(shards, mesh=mesh, in_specs=in_specs, out_specs=out_specs, check_vma=False)
```

time: 707 us -> 89.5 us (0.13); the launches traced: 698 us -> 89.3 us
  blocking collectives: 586 us -> 0 us
  matrix products: 54.8 us -> 0 us
  waiting for transfers between devices: 0 us -> 34.3 us
  other arithmetic: 28.4 us -> 0 us
  Pallas kernels: 0 us -> 26.3 us
  starting transfers between devices: 0 us -> 22.4 us
  local copies, waits for them, and re-layouts: 23.1 us -> 6.22 us
    all_gather x8 -> x0, blocking collectives: 544 us -> none  [settle(): lax.all_gather((node_marks,) + head_rows + tail_only, ('row', 'col'), axi...]
    dot_general x12 -> x0, matrix products: 54.8 us -> none  [the longest x4 30.3 us: lifted_terms(): spread = jnp.dot(block, flat_frames, preferred_element_type=jnp.float32)]
    unnamed x1 -> x0, blocking collectives: 42.1 us -> none
    ppermute x0 -> x21, waiting for transfers between devices: none -> 34.3 us  [swap(): groups.append(lax.ppermute(value, ('row', 'col'), pairs))]
    pallas_call x0 -> x10, Pallas kernels: none -> 26.3 us  [run(): pl.pallas_call(kernel, out_shape=outs, in_specs=[vmem] * len(args), out_s...]
    ppermute x0 -> x21, starting transfers between devices: none -> 22.4 us  [swap(): groups.append(lax.ppermute(value, ('row', 'col'), pairs))]
    reduce_sum x51 -> x0, other arithmetic: 14.4 us -> none  [the longest x33 7.54 us: orthonormal(): vector = vector - jnp.sum(column * vector) * column]
    reshape x3 -> x0, local copies, waits for them, and re-layouts: 8.32 us -> none  [settle(): flat_parts = [piece.reshape(piece.shape[0], -1) for piece in pieces]]
  transfers between devices with their start and end apart: 0 -> 21, of which waited for: 0 -> 19; matrix products, arithmetic and copies ran while one was open for 0% -> 0% of each run, Pallas kernels for 0% -> 0%
where the time goes in v1:
time: 89.5 us; the launch traced here: 89.3 us
  waiting for transfers between devices  34.3 us (38%)
  Pallas kernels  26.3 us (29%)
  starting transfers between devices  22.4 us (25%)
  local copies, waits for them, and re-layouts  6.22 us (7%)
    ppermute x21, waiting for transfers between devices, swap(): groups.append(lax.ppermute(value, ('row', 'col'), pairs))  34.3 us
    pallas_call x10, Pallas kernels, run(): pl.pallas_call(kernel, out_shape=outs, in_specs=[vmem] * len(args), out_s...  26.3 us
    ppermute x21, starting transfers between devices, swap(): groups.append(lax.ppermute(value, ('row', 'col'), pairs))  22.4 us
    unnamed x5, local copies, waits for them, and re-layouts  6.22 us
  transfers between devices with their start and end apart: 21, of which 19 were waited for; matrix products, arithmetic and copies ran while one was open for 0% of the time, Pallas kernels for 0%

profile of v1, /device:TPU:0, one launch (start us, length us, event | category | flops | bytes accessed | tf_op | source)
XLA Modules:
  0.0 89.3 jit_solution(9362170644165708929)
XLA Ops:
  0.0 0.9 copy.4.init_ref
  0.9 4.6 %copy-done = bf16[8192,768]{1,0:T(8,128)(2,1)S(1)} copy-done((bf16[8192,768]{1,0:T(8,128)(2,1)S(1)}, bf16[8192,768]{1,0:T(8,128)(2,1)}, u32[]{:S(2)}) %copy-start) | copy-done | bytes 12582936
  5.5 0.8 copy-done.1
  6.2 5.8 %shard_map.37 = (f32[64,896]{1,0:T(8,128)S(1)}, f32[8,896]{1,0:T(8,128)S(1)}, f32[24,896]{1,0:T(8,128)S(1)}) custom-call(bf16[8192,768]{1,0:T(8,128)(2,1)S(1)} %copy-done, s32[1,8192]{1,0:T(1,128)S(1)} %bitcast.1, f32[768,8]{1,0:T(8,128)S(1)} %copy.4.init_ref), custom_call_target="tpu_custom_call" | custom-call | tf_op jit(solution)/shard_map/pallas_call | solution.py:386
  12.0 3.0 %collective-permute-start = (f32[24,896]{1,0:T(8,128)S(1)}, f32[24,896]{1,0:T(8,128)S(1)}, u32[]{:S(2)}, u32[]{:S(2)}) collective-permute-start(f32[24,896]{1,0:T(8,128)S(1)} %get-tuple-element.30.own_ref.refs_0_), channel_id=1, source_target_pairs={{0,1},{1,0},{2,3},{3,2},{4,5},{5,4},{6,7},{7,6},{8,9},{9,8},{10,11... | collective-permute-start | bytes 258056 | tf_op jit(solution)/shard_map/ppermute | solution.py:374
  15.1 2.5 %collective-permute-done.refs_1_ = f32[24,896]{1,0:T(8,128)S(1)} collective-permute-done((f32[24,896]{1,0:T(8,128)S(1)}, f32[24,896]{1,0:T(8,128)S(1)}, u32[]{:S(2)}, u32[]{:S(2)}) %collective-permute-start) | collective-permute-done | bytes 86048 | tf_op jit(solution)/shard_map/ppermute | solution.py:374
  17.6 0.1 shard_map.38
  17.7 4.1 %collective-permute-start.3 = (f32[24,896]{1,0:T(8,128)S(1)}, f32[24,896]{1,0:T(8,128)S(1)}, u32[]{:S(2)}, u32[]{:S(2)}) collective-permute-start(f32[24,896]{1,0:T(8,128)S(1)} %get-tuple-element.32.refs_0_), channel_id=1, source_target_pairs={{0,6},{1,7},{2,0},{3,1},{4,2},{5,3},{6,4},{7,5},{8,14},{9,15},{10,... | collective-permute-start | bytes 258056 | tf_op jit(solution)/shard_map/ppermute | solution.py:374
  21.8 1.0 %collective-permute-start.1 = (f32[24,896]{1,0:T(8,128)S(1)}, f32[24,896]{1,0:T(8,128)S(1)}, u32[]{:S(2)}, u32[]{:S(2)}) collective-permute-start(f32[24,896]{1,0:T(8,128)S(1)} %get-tuple-element.32.refs_0_), channel_id=1, source_target_pairs={{0,2},{1,3},{2,4},{3,5},{4,6},{5,7},{6,0},{7,1},{8,10},{9,11},{10,... | collective-permute-start | bytes 258056 | tf_op jit(solution)/shard_map/ppermute | solution.py:374
  22.8 1.5 %collective-permute-done.3.refs_3_ = f32[24,896]{1,0:T(8,128)S(1)} collective-permute-done((f32[24,896]{1,0:T(8,128)S(1)}, f32[24,896]{1,0:T(8,128)S(1)}, u32[]{:S(2)}, u32[]{:S(2)}) %collective-permute-start.3) | collective-permute-done | bytes 86048 | tf_op jit(solution)/shard_map/ppermute | solution.py:374
  24.3 4.5 %collective-permute-done.2.refs_2_ = f32[24,896]{1,0:T(8,128)S(1)} collective-permute-done((f32[24,896]{1,0:T(8,128)S(1)}, f32[24,896]{1,0:T(8,128)S(1)}, u32[]{:S(2)}, u32[]{:S(2)}) %collective-permute-start.2) | collective-permute-done | bytes 86048 | tf_op jit(solution)/shard_map/ppermute | solution.py:374
  28.9 0.1 shard_map.39
  29.0 0.7 collective-permute-start.6
  29.7 0.9 %collective-permute-start.5 = (f32[24,896]{1,0:T(8,128)S(1)}, f32[24,896]{1,0:T(8,128)S(1)}, u32[]{:S(2)}, u32[]{:S(2)}) collective-permute-start(f32[24,896]{1,0:T(8,128)S(1)} %get-tuple-element.34.refs_0_), channel_id=1, source_target_pairs={{0,16},{1,17},{2,18},{3,19},{4,20},{5,21},{6,22},{7,23},{8,24},{9,... | collective-permute-start | bytes 258056 | tf_op jit(solution)/shard_map/ppermute | solution.py:374
  30.7 0.2 collective-permute-start.4
  30.8 1.5 %collective-permute-done.6.refs_3_ = f32[24,896]{1,0:T(8,128)S(1)} collective-permute-done((f32[24,896]{1,0:T(8,128)S(1)}, f32[24,896]{1,0:T(8,128)S(1)}, u32[]{:S(2)}, u32[]{:S(2)}) %collective-permute-start.6) | collective-permute-done | bytes 86048 | tf_op jit(solution)/shard_map/ppermute | solution.py:374
  32.3 3.5 %collective-permute-done.5.refs_2_ = f32[24,896]{1,0:T(8,128)S(1)} collective-permute-done((f32[24,896]{1,0:T(8,128)S(1)}, f32[24,896]{1,0:T(8,128)S(1)}, u32[]{:S(2)}, u32[]{:S(2)}) %collective-permute-start.5) | collective-permute-done | bytes 86048 | tf_op jit(solution)/shard_map/ppermute | solution.py:374
  35.8 7.3 %shard_map.40 = (f32[64,768]{1,0:T(8,128)S(1)}, f32[16,768]{1,0:T(8,128)S(1)}, f32[8,768]{1,0:T(8,128)S(1)}, f32[32,128]{1,0:T(8,128)S(1)}) custom-call(bf16[8192,768]{1,0:T(8,128)(2,1)S(1)} %copy-done, s32[1,8192]{1,0:T(1,128)S(1)} %bitcast.2, f32[64,896]{1,0:T(8,128)S(1)} %get-tuple-element.28.part_ref, f32[8,896]{1,0:T(8,128)S(1)} %get-tuple-element.29.sums_ref, ...), custom_call_target="tpu_custom_call" | custom-call | tf_op jit(solution)/shard_map/pallas_call | solution.py:386
  43.1 1.6 %collective-permute-start.7 = (f32[16,768]{1,0:T(8,128)S(1)}, f32[16,768]{1,0:T(8,128)S(1)}, u32[]{:S(2)}, u32[]{:S(2)}) collective-permute-start(f32[16,768]{1,0:T(8,128)S(1)} %get-tuple-element.37.own_ref.refs_0_), channel_id=1, source_target_pairs={{0,1},{1,0},{2,3},{3,2},{4,5},{5,4},{6,7},{7,6},{8,9},{9,8},{10,11... | collective-permute-start | bytes 147464 | tf_op jit(solution)/shard_map/ppermute | solution.py:374
  44.6 2.6 %collective-permute-done.7.refs_1_ = f32[16,768]{1,0:T(8,128)S(1)} collective-permute-done((f32[16,768]{1,0:T(8,128)S(1)}, f32[16,768]{1,0:T(8,128)S(1)}, u32[]{:S(2)}, u32[]{:S(2)}) %collective-permute-start.7) | collective-permute-done | bytes 49184 | tf_op jit(solution)/shard_map/ppermute | solution.py:374
  47.3 1.8 %collective-permute-start.10 = (f32[16,768]{1,0:T(8,128)S(1)}, f32[16,768]{1,0:T(8,128)S(1)}, u32[]{:S(2)}, u32[]{:S(2)}) collective-permute-start(f32[16,768]{1,0:T(8,128)S(1)} %get-tuple-element.41.refs_0_), channel_id=1, source_target_pairs={{0,6},{1,7},{2,0},{3,1},{4,2},{5,3},{6,4},{7,5},{8,14},{9,15},{10,... | collective-permute-start | bytes 147464 | tf_op jit(solution)/shard_map/ppermute | solution.py:374
  49.0 0.1 collective-permute-start.9
  49.2 1.9 %collective-permute-start.8 = (f32[16,768]{1,0:T(8,128)S(1)}, f32[16,768]{1,0:T(8,128)S(1)}, u32[]{:S(2)}, u32[]{:S(2)}) collective-permute-start(f32[16,768]{1,0:T(8,128)S(1)} %get-tuple-element.41.refs_0_), channel_id=1, source_target_pairs={{0,2},{1,3},{2,4},{3,5},{4,6},{5,7},{6,0},{7,1},{8,10},{9,11},{10,... | collective-permute-start | bytes 147464 | tf_op jit(solution)/shard_map/ppermute | solution.py:374
  51.1 0.6 collective-permute-done.10.refs_3_
  51.7 2.6 %collective-permute-done.9.refs_2_ = f32[16,768]{1,0:T(8,128)S(1)} collective-permute-done((f32[16,768]{1,0:T(8,128)S(1)}, f32[16,768]{1,0:T(8,128)S(1)}, u32[]{:S(2)}, u32[]{:S(2)}) %collective-permute-start.9) | collective-permute-done | bytes 49184 | tf_op jit(solution)/shard_map/ppermute | solution.py:374
  54.3 0.7 collective-permute-done.8.refs_1_
  55.1 0.1 shard_map.42
  55.2 0.9 %collective-permute-start.12 = (f32[16,768]{1,0:T(8,128)S(1)}, f32[16,768]{1,0:T(8,128)S(1)}, u32[]{:S(2)}, u32[]{:S(2)}) collective-permute-start(f32[16,768]{1,0:T(8,128)S(1)} %get-tuple-element.44.refs_0_), channel_id=1, source_target_pairs={{0,16},{1,17},{2,18},{3,19},{4,20},{5,21},{6,22},{7,23},{8,24},{9,... | collective-permute-start | bytes 147464 | tf_op jit(solution)/shard_map/ppermute | solution.py:374
  56.1 0.2 collective-permute-start.11
  56.3 0.8 collective-permute-done.13.refs_3_
  57.0 2.6 %collective-permute-done.12.refs_2_ = f32[16,768]{1,0:T(8,128)S(1)} collective-permute-done((f32[16,768]{1,0:T(8,128)S(1)}, f32[16,768]{1,0:T(8,128)S(1)}, u32[]{:S(2)}, u32[]{:S(2)}) %collective-permute-start.12) | collective-permute-done | bytes 49184 | tf_op jit(solution)/shard_map/ppermute | solution.py:374
  59.6 0.3 collective-permute-done.11.refs_1_
  59.9 7.2 %shard_map.43 = (f32[64,768]{1,0:T(8,128)S(1)}, f32[16,768]{1,0:T(8,128)S(1)}) custom-call(bf16[8192,768]{1,0:T(8,128)(2,1)S(1)} %copy-done, s32[1,8192]{1,0:T(1,128)S(1)} %bitcast.3, f32[64,768]{1,0:T(8,128)S(1)} %get-tuple-element.35.part_ref, f32[8,768]{1,0:T(8,128)S(1)} %get-tuple-element.36.centre_ref, f32[16,768]{1,0:T(8,128)S(1)} %get-tuple-element.42.own_ref, ...), custom_call_target="tpu_custom_call" | custom-call | tf_op jit(solution)/shard_map/pallas_call | solution.py:386
  67.1 1.6 %collective-permute-start.14 = (f32[16,768]{1,0:T(8,128)S(1)}, f32[16,768]{1,0:T(8,128)S(1)}, u32[]{:S(2)}, u32[]{:S(2)}) collective-permute-start(f32[16,768]{1,0:T(8,128)S(1)} %get-tuple-element.46.own_ref.refs_0_), channel_id=1, source_target_pairs={{0,1},{1,0},{2,3},{3,2},{4,5},{5,4},{6,7},{7,6},{8,9},{9,8},{10,11... | collective-permute-start | bytes 147464 | tf_op jit(solution)/shard_map/ppermute | solution.py:374
  68.6 2.6 %collective-permute-done.14.refs_1_ = f32[16,768]{1,0:T(8,128)S(1)} collective-permute-done((f32[16,768]{1,0:T(8,128)S(1)}, f32[16,768]{1,0:T(8,128)S(1)}, u32[]{:S(2)}, u32[]{:S(2)}) %collective-permute-start.14) | collective-permute-done | bytes 49184 | tf_op jit(solution)/shard_map/ppermute | solution.py:374
  71.3 1.3 %collective-permute-start.17 = (f32[16,768]{1,0:T(8,128)S(1)}, f32[16,768]{1,0:T(8,128)S(1)}, u32[]{:S(2)}, u32[]{:S(2)}) collective-permute-start(f32[16,768]{1,0:T(8,128)S(1)} %get-tuple-element.48.refs_0_), channel_id=1, source_target_pairs={{0,6},{1,7},{2,0},{3,1},{4,2},{5,3},{6,4},{7,5},{8,14},{9,15},{10,... | collective-permute-start | bytes 147464 | tf_op jit(solution)/shard_map/ppermute | solution.py:374
  72.6 0.3 collective-permute-start.16
  73.0 1.4 %collective-permute-start.15 = (f32[16,768]{1,0:T(8,128)S(1)}, f32[16,768]{1,0:T(8,128)S(1)}, u32[]{:S(2)}, u32[]{:S(2)}) collective-permute-start(f32[16,768]{1,0:T(8,128)S(1)} %get-tuple-element.48.refs_0_), channel_id=1, source_target_pairs={{0,2},{1,3},{2,4},{3,5},{4,6},{5,7},{6,0},{7,1},{8,10},{9,11},{10,... | collective-permute-start | bytes 147464 | tf_op jit(solution)/shard_map/ppermute | solution.py:374
  74.4 1.2 %collective-permute-done.17.refs_3_ = f32[16,768]{1,0:T(8,128)S(1)} collective-permute-done((f32[16,768]{1,0:T(8,128)S(1)}, f32[16,768]{1,0:T(8,128)S(1)}, u32[]{:S(2)}, u32[]{:S(2)}) %collective-permute-start.17) | collective-permute-done | bytes 49184 | tf_op jit(solution)/shard_map/ppermute | solution.py:374
  75.6 2.6 %collective-permute-done.16.refs_2_ = f32[16,768]{1,0:T(8,128)S(1)} collective-permute-done((f32[16,768]{1,0:T(8,128)S(1)}, f32[16,768]{1,0:T(8,128)S(1)}, u32[]{:S(2)}, u32[]{:S(2)}) %collective-permute-start.16) | collective-permute-done | bytes 49184 | tf_op jit(solution)/shard_map/ppermute | solution.py:374
  78.1 0.7 collective-permute-done.15.refs_1_
  78.8 0.1 shard_map.45
  79.0 1.0 %collective-permute-start.19 = (f32[16,768]{1,0:T(8,128)S(1)}, f32[16,768]{1,0:T(8,128)S(1)}, u32[]{:S(2)}, u32[]{:S(2)}) collective-permute-start(f32[16,768]{1,0:T(8,128)S(1)} %get-tuple-element.50.refs_0_), channel_id=1, source_target_pairs={{0,16},{1,17},{2,18},{3,19},{4,20},{5,21},{6,22},{7,23},{8,24},{9,... | collective-permute-start | bytes 147464 | tf_op jit(solution)/shard_map/ppermute | solution.py:374
  80.0 0.2 collective-permute-start.18
  80.2 0.5 collective-permute-done.20.refs_3_
  80.7 2.6 %collective-permute-done.19.refs_2_ = f32[16,768]{1,0:T(8,128)S(1)} collective-permute-done((f32[16,768]{1,0:T(8,128)S(1)}, f32[16,768]{1,0:T(8,128)S(1)}, u32[]{:S(2)}, u32[]{:S(2)}) %collective-permute-start.19) | collective-permute-done | bytes 49184 | tf_op jit(solution)/shard_map/ppermute | solution.py:374
  83.4 0.3 collective-permute-done.18.refs_1_
  83.7 5.6 %shard_map.46 = f32[8,8192]{1,0:T(8,128)} custom-call(bf16[8192,768]{1,0:T(8,128)(2,1)S(1)} %copy-done, s32[1,8192]{1,0:T(1,128)S(1)} %bitcast.4, f32[64,768]{1,0:T(8,128)S(1)} %get-tuple-element.45.part_ref, f32[8,768]{1,0:T(8,128)S(1)} %get-tuple-element.36.centre_ref, f32[16,768]{1,0:T(8,128)S(1)} %get-tuple-element.49.own_ref, ...), custom_call_target="tpu_custom_call" | custom-call | tf_op jit(solution)/shard_map/pallas_call | solution.py:386
  (9 shorter events, 0.3 us)
Async XLA Ops:
  0.9 4.6 %copy-start = (bf16[8192,768]{1,0:T(8,128)(2,1)S(1)}, bf16[8192,768]{1,0:T(8,128)(2,1)}, u32[]{:S(2)}) copy-start(bf16[8192,768]{1,0:T(8,128)(2,1)} %points_ref.7) | copy-start | bytes 37748740
  5.5 0.8 copy-start.1
  12.0 5.5 %collective-permute-start = (f32[24,896]{1,0:T(8,128)S(1)}, f32[24,896]{1,0:T(8,128)S(1)}, u32[]{:S(2)}, u32[]{:S(2)}) collective-permute-start(f32[24,896]{1,0:T(8,128)S(1)} %get-tuple-element.30.own_ref.refs_0_), channel_id=1, source_target_pairs={{0,1},{1,0},{2,3},{3,2},{4,5},{5,4},{6,7},{7,6},{8,9},{9,8},{10,11... | collective-permute-start | bytes 258056 | tf_op jit(solution)/shard_map/ppermute | solution.py:374
  17.7 6.7 %collective-permute-start.3 = (f32[24,896]{1,0:T(8,128)S(1)}, f32[24,896]{1,0:T(8,128)S(1)}, u32[]{:S(2)}, u32[]{:S(2)}) collective-permute-start(f32[24,896]{1,0:T(8,128)S(1)} %get-tuple-element.32.refs_0_), channel_id=1, source_target_pairs={{0,6},{1,7},{2,0},{3,1},{4,2},{5,3},{6,4},{7,5},{8,14},{9,15},{10,... | collective-permute-start | bytes 258056 | tf_op jit(solution)/shard_map/ppermute | solution.py:374
  21.8 7.1 %collective-permute-start.2 = (f32[24,896]{1,0:T(8,128)S(1)}, f32[24,896]{1,0:T(8,128)S(1)}, u32[]{:S(2)}, u32[]{:S(2)}) collective-permute-start(f32[24,896]{1,0:T(8,128)S(1)} %get-tuple-element.32.refs_0_), channel_id=1, source_target_pairs={{0,4},{1,5},{2,6},{3,7},{4,0},{5,1},{6,2},{7,3},{8,12},{9,13},{10,... | collective-permute-start | bytes 258056 | tf_op jit(solution)/shard_map/ppermute | solution.py:374
  21.8 7.1 %collective-permute-start.1 = (f32[24,896]{1,0:T(8,128)S(1)}, f32[24,896]{1,0:T(8,128)S(1)}, u32[]{:S(2)}, u32[]{:S(2)}) collective-permute-start(f32[24,896]{1,0:T(8,128)S(1)} %get-tuple-element.32.refs_0_), channel_id=1, source_target_pairs={{0,2},{1,3},{2,4},{3,5},{4,6},{5,7},{6,0},{7,1},{8,10},{9,11},{10,... | collective-permute-start | bytes 258056 | tf_op jit(solution)/shard_map/ppermute | solution.py:374
  29.0 3.3 %collective-permute-start.6 = (f32[24,896]{1,0:T(8,128)S(1)}, f32[24,896]{1,0:T(8,128)S(1)}, u32[]{:S(2)}, u32[]{:S(2)}) collective-permute-start(f32[24,896]{1,0:T(8,128)S(1)} %get-tuple-element.34.refs_0_), channel_id=1, source_target_pairs={{0,24},{1,25},{2,26},{3,27},{4,28},{5,29},{6,30},{7,31},{8,0},{9,1... | collective-permute-start | bytes 258056 | tf_op jit(solution)/shard_map/ppermute | solution.py:374
  29.7 6.0 %collective-permute-start.5 = (f32[24,896]{1,0:T(8,128)S(1)}, f32[24,896]{1,0:T(8,128)S(1)}, u32[]{:S(2)}, u32[]{:S(2)}) collective-permute-start(f32[24,896]{1,0:T(8,128)S(1)} %get-tuple-element.34.refs_0_), channel_id=1, source_target_pairs={{0,16},{1,17},{2,18},{3,19},{4,20},{5,21},{6,22},{7,23},{8,24},{9,... | collective-permute-start | bytes 258056 | tf_op jit(solution)/shard_map/ppermute | solution.py:374
  30.7 5.2 %collective-permute-start.4 = (f32[24,896]{1,0:T(8,128)S(1)}, f32[24,896]{1,0:T(8,128)S(1)}, u32[]{:S(2)}, u32[]{:S(2)}) collective-permute-start(f32[24,896]{1,0:T(8,128)S(1)} %get-tuple-element.34.refs_0_), channel_id=1, source_target_pairs={{0,8},{1,9},{2,10},{3,11},{4,12},{5,13},{6,14},{7,15},{8,16},{9,17... | collective-permute-start | bytes 258056 | tf_op jit(solution)/shard_map/ppermute | solution.py:374
  43.1 4.2 %collective-permute-start.7 = (f32[16,768]{1,0:T(8,128)S(1)}, f32[16,768]{1,0:T(8,128)S(1)}, u32[]{:S(2)}, u32[]{:S(2)}) collective-permute-start(f32[16,768]{1,0:T(8,128)S(1)} %get-tuple-element.37.own_ref.refs_0_), channel_id=1, source_target_pairs={{0,1},{1,0},{2,3},{3,2},{4,5},{5,4},{6,7},{7,6},{8,9},{9,8},{10,11... | collective-permute-start | bytes 147464 | tf_op jit(solution)/shard_map/ppermute | solution.py:374
  47.3 4.4 %collective-permute-start.10 = (f32[16,768]{1,0:T(8,128)S(1)}, f32[16,768]{1,0:T(8,128)S(1)}, u32[]{:S(2)}, u32[]{:S(2)}) collective-permute-start(f32[16,768]{1,0:T(8,128)S(1)} %get-tuple-element.41.refs_0_), channel_id=1, source_target_pairs={{0,6},{1,7},{2,0},{3,1},{4,2},{5,3},{6,4},{7,5},{8,14},{9,15},{10,... | collective-permute-start | bytes 147464 | tf_op jit(solution)/shard_map/ppermute | solution.py:374
  49.0 5.3 %collective-permute-start.9 = (f32[16,768]{1,0:T(8,128)S(1)}, f32[16,768]{1,0:T(8,128)S(1)}, u32[]{:S(2)}, u32[]{:S(2)}) collective-permute-start(f32[16,768]{1,0:T(8,128)S(1)} %get-tuple-element.41.refs_0_), channel_id=1, source_target_pairs={{0,4},{1,5},{2,6},{3,7},{4,0},{5,1},{6,2},{7,3},{8,12},{9,13},{10,... | collective-permute-start | bytes 147464 | tf_op jit(solution)/shard_map/ppermute | solution.py:374
  49.2 5.9 %collective-permute-start.8 = (f32[16,768]{1,0:T(8,128)S(1)}, f32[16,768]{1,0:T(8,128)S(1)}, u32[]{:S(2)}, u32[]{:S(2)}) collective-permute-start(f32[16,768]{1,0:T(8,128)S(1)} %get-tuple-element.41.refs_0_), channel_id=1, source_target_pairs={{0,2},{1,3},{2,4},{3,5},{4,6},{5,7},{6,0},{7,1},{8,10},{9,11},{10,... | collective-permute-start | bytes 147464 | tf_op jit(solution)/shard_map/ppermute | solution.py:374
  55.1 1.9 %collective-permute-start.13 = (f32[16,768]{1,0:T(8,128)S(1)}, f32[16,768]{1,0:T(8,128)S(1)}, u32[]{:S(2)}, u32[]{:S(2)}) collective-permute-start(f32[16,768]{1,0:T(8,128)S(1)} %get-tuple-element.44.refs_0_), channel_id=1, source_target_pairs={{0,24},{1,25},{2,26},{3,27},{4,28},{5,29},{6,30},{7,31},{8,0},{9,1... | collective-permute-start | bytes 147464 | tf_op jit(solution)/shard_map/ppermute | solution.py:374
  55.2 4.4 %collective-permute-start.12 = (f32[16,768]{1,0:T(8,128)S(1)}, f32[16,768]{1,0:T(8,128)S(1)}, u32[]{:S(2)}, u32[]{:S(2)}) collective-permute-start(f32[16,768]{1,0:T(8,128)S(1)} %get-tuple-element.44.refs_0_), channel_id=1, source_target_pairs={{0,16},{1,17},{2,18},{3,19},{4,20},{5,21},{6,22},{7,23},{8,24},{9,... | collective-permute-start | bytes 147464 | tf_op jit(solution)/shard_map/ppermute | solution.py:374
  56.1 3.8 %collective-permute-start.11 = (f32[16,768]{1,0:T(8,128)S(1)}, f32[16,768]{1,0:T(8,128)S(1)}, u32[]{:S(2)}, u32[]{:S(2)}) collective-permute-start(f32[16,768]{1,0:T(8,128)S(1)} %get-tuple-element.44.refs_0_), channel_id=1, source_target_pairs={{0,8},{1,9},{2,10},{3,11},{4,12},{5,13},{6,14},{7,15},{8,16},{9,17... | collective-permute-start | bytes 147464 | tf_op jit(solution)/shard_map/ppermute | solution.py:374
  67.1 4.2 %collective-permute-start.14 = (f32[16,768]{1,0:T(8,128)S(1)}, f32[16,768]{1,0:T(8,128)S(1)}, u32[]{:S(2)}, u32[]{:S(2)}) collective-permute-start(f32[16,768]{1,0:T(8,128)S(1)} %get-tuple-element.46.own_ref.refs_0_), channel_id=1, source_target_pairs={{0,1},{1,0},{2,3},{3,2},{4,5},{5,4},{6,7},{7,6},{8,9},{9,8},{10,11... | collective-permute-start | bytes 147464 | tf_op jit(solution)/shard_map/ppermute | solution.py:374
  71.3 4.3 %collective-permute-start.17 = (f32[16,768]{1,0:T(8,128)S(1)}, f32[16,768]{1,0:T(8,128)S(1)}, u32[]{:S(2)}, u32[]{:S(2)}) collective-permute-start(f32[16,768]{1,0:T(8,128)S(1)} %get-tuple-element.48.refs_0_), channel_id=1, source_target_pairs={{0,6},{1,7},{2,0},{3,1},{4,2},{5,3},{6,4},{7,5},{8,14},{9,15},{10,... | collective-permute-start | bytes 147464 | tf_op jit(solution)/shard_map/ppermute | solution.py:374
  72.6 5.5 %collective-permute-start.16 = (f32[16,768]{1,0:T(8,128)S(1)}, f32[16,768]{1,0:T(8,128)S(1)}, u32[]{:S(2)}, u32[]{:S(2)}) collective-permute-start(f32[16,768]{1,0:T(8,128)S(1)} %get-tuple-element.48.refs_0_), channel_id=1, source_target_pairs={{0,4},{1,5},{2,6},{3,7},{4,0},{5,1},{6,2},{7,3},{8,12},{9,13},{10,... | collective-permute-start | bytes 147464 | tf_op jit(solution)/shard_map/ppermute | solution.py:374
  73.0 5.9 %collective-permute-start.15 = (f32[16,768]{1,0:T(8,128)S(1)}, f32[16,768]{1,0:T(8,128)S(1)}, u32[]{:S(2)}, u32[]{:S(2)}) collective-permute-start(f32[16,768]{1,0:T(8,128)S(1)} %get-tuple-element.48.refs_0_), channel_id=1, source_target_pairs={{0,2},{1,3},{2,4},{3,5},{4,6},{5,7},{6,0},{7,1},{8,10},{9,11},{10,... | collective-permute-start | bytes 147464 | tf_op jit(solution)/shard_map/ppermute | solution.py:374
  78.9 1.8 %collective-permute-start.20 = (f32[16,768]{1,0:T(8,128)S(1)}, f32[16,768]{1,0:T(8,128)S(1)}, u32[]{:S(2)}, u32[]{:S(2)}) collective-permute-start(f32[16,768]{1,0:T(8,128)S(1)} %get-tuple-element.50.refs_0_), channel_id=1, source_target_pairs={{0,24},{1,25},{2,26},{3,27},{4,28},{5,29},{6,30},{7,31},{8,0},{9,1... | collective-permute-start | bytes 147464 | tf_op jit(solution)/shard_map/ppermute | solution.py:374
  79.0 4.4 %collective-permute-start.19 = (f32[16,768]{1,0:T(8,128)S(1)}, f32[16,768]{1,0:T(8,128)S(1)}, u32[]{:S(2)}, u32[]{:S(2)}) collective-permute-start(f32[16,768]{1,0:T(8,128)S(1)} %get-tuple-element.50.refs_0_), channel_id=1, source_target_pairs={{0,16},{1,17},{2,18},{3,19},{4,20},{5,21},{6,22},{7,23},{8,24},{9,... | collective-permute-start | bytes 147464 | tf_op jit(solution)/shard_map/ppermute | solution.py:374
  80.0 3.6 %collective-permute-start.18 = (f32[16,768]{1,0:T(8,128)S(1)}, f32[16,768]{1,0:T(8,128)S(1)}, u32[]{:S(2)}, u32[]{:S(2)}) collective-permute-start(f32[16,768]{1,0:T(8,128)S(1)} %get-tuple-element.50.refs_0_), channel_id=1, source_target_pairs={{0,8},{1,9},{2,10},{3,11},{4,12},{5,13},{6,14},{7,15},{8,16},{9,17... | collective-permute-start | bytes 147464 | tf_op jit(solution)/shard_map/ppermute | solution.py:374

commit v2 on v1

--- a/solution.py
+++ b/solution.py
@@ -10,7 +10,11 @@
 ITERS = 3
 SLOTS = 8
 LANES = 128
-BLOCK = 1024
+BLOCK = 2048
+PIECE = 1024
+AHEAD = 3
+FIRST = 1024
+STEP = 2048
 F32 = jnp.float32
 BF16 = jnp.bfloat16
 MIB = 1 << 20
@@ -63,60 +67,89 @@
 
 
 def ends_of(nodes_ref):
-    nodes = nodes_ref[...]
-    return jnp.min(nodes), jnp.max(nodes)
-
-
-def first_sweep_kernel(axes, points_ref, nodes_ref, init_ref, part_ref, sums_ref, note_ref):
+    rows = nodes_ref.shape[1]
+    return jnp.min(nodes_ref[:, :LANES]), jnp.max(nodes_ref[:, rows - LANES :])
+
+
+def tile_of(sums, counts, first, last):
+    width = sums.shape[1]
+    pieces = [sums[:, at : at + LANES] for at in range(0, width, LANES)]
+    left = lax.broadcasted_iota(jnp.int32, (1, LANES), 1) < LANES // 2
+    return jnp.concatenate(pieces + [counts, jnp.where(left, first, last)], 0)
+
+
+def sums_of(tile, width):
+    return jnp.concatenate([tile[row : row + 1] for row in range(width // LANES)], 1)
+
+
+def cuts_of(rows):
+    return [0] + list(range(FIRST, rows - 1, STEP)) + [rows]
+
+
+def first_sweep_kernel(axes, points_hbm, nodes_hbm, init_hbm, part_ref, sums_ref, note_ref, points_ref, nodes_ref, init_ref, sems):
     rows, width = points_ref.shape
+    small = [
+        pltpu.make_async_copy(nodes_hbm, nodes_ref, sems.at[0]),
+        pltpu.make_async_copy(init_hbm, init_ref, sems.at[1]),
+    ]
+    cuts = cuts_of(rows)
+    copies = []
+    for start, stop in zip(cuts[:-1], cuts[1:]):
+        at = pl.ds(start, stop - start)
+        sem = sems.at[2 + len(copies)]
+        copies.append(pltpu.make_async_copy(points_hbm.at[at], points_ref.at[at], sem))
+    for copy in small + copies[:AHEAD]:
+        copy.start()
+    for copy in small:
+        copy.wait()
     first, last = ends_of(nodes_ref)
-    frame = init_ref[...].T.astype(BF16)
+    frame = init_ref[...].astype(BF16)
     slot_rows = SLOTS * axes
     moment = jnp.zeros((2 * slot_rows + SLOTS, width), F32)
-    columns = jnp.zeros((slot_rows, LANES), F32)
     counts = jnp.zeros((SLOTS, LANES), F32)
-    for start in range(0, rows, BLOCK):
-        block = points_ref[start : start + BLOCK, :]
-        slot_of = nodes_ref[:, start : start + BLOCK] - first
+    left = block = None
+    for start in range(0, rows, PIECE):
+        if start in cuts:
+            piece = cuts.index(start)
+            copies[piece].wait()
+            if piece + AHEAD < len(copies):
+                copies[piece + AHEAD].start()
+        before, left_before = block, left
+        block = points_ref[start : start + PIECE, :]
         spread = dot_nt(frame, block)
+        if start > 0:
+            moment = moment + dot_nn(left_before, before)
+        slot_of = nodes_ref[:, start : start + PIECE] - first
         high = spread.astype(BF16).astype(F32)
-        low = (spread - high).astype(BF16).astype(F32)
+        low = spread - high
         highs = []
         lows = []
         for slot in range(SLOTS):
             here = slot_of == slot
             highs.append(jnp.where(here, high, 0.0))
             lows.append(jnp.where(here, low, 0.0))
-        highs = jnp.concatenate(highs, 0)
-        lows = jnp.concatenate(lows, 0)
-        member = (slot_of == lax.broadcasted_iota(jnp.int32, (SLOTS, BLOCK), 0)).astype(F32)
-        left = jnp.concatenate([highs.astype(BF16), lows.astype(BF16), member.astype(BF16)], 0)
-        moment = moment + dot_nn(left, block)
-        columns = columns + fold_lanes(highs + lows)
+        member = (slot_of == lax.broadcasted_iota(jnp.int32, (SLOTS, PIECE), 0)).astype(F32)
+        left = jnp.concatenate(highs + lows + [member], 0).astype(BF16)
         counts = counts + fold_lanes(member)
-    part_ref[:, :width] = moment[:slot_rows] + moment[slot_rows : 2 * slot_rows]
-    part_ref[:, width:] = jnp.broadcast_to(jnp.sum(columns, 1, keepdims=True), columns.shape)
+    moment = moment + dot_nn(left, block)
+    part_ref[...] = moment[:slot_rows] + moment[slot_rows : 2 * slot_rows]
     sums_ref[:, :width] = moment[2 * slot_rows :]
     sums_ref[:, width:] = jnp.broadcast_to(jnp.sum(counts, 1, keepdims=True), counts.shape)
     span = last - first
-    tail = pl.multiple_of(span * axes, axes)
-    note_ref[:axes, :] = part_ref[:axes, :]
-    note_ref[axes : 2 * axes, :] = part_ref[pl.ds(tail, axes), :]
-    base = 2 * axes
-    wide = sums_ref.shape[1]
-    note_ref[base : base + 1, :] = sums_ref[0:1, :]
-    note_ref[base + 1 : base + 2, :] = sums_ref[pl.ds(span, 1), :]
-    note_ref[base + 2 : base + 3, :] = jnp.full((1, wide), first.astype(F32))
-    note_ref[base + 3 : base + 4, :] = jnp.full((1, wide), last.astype(F32))
-    note_ref[base + 4 :, :] = jnp.zeros((4, wide), F32)
+    ids = (first.astype(F32), last.astype(F32))
+    for at, slot in ((0, 0), (axes, span)):
+        own = sums_ref[pl.ds(slot, 1), :]
+        note_ref[at : at + axes, :width] = part_ref[pl.ds(pl.multiple_of(slot * axes, axes), axes), :]
+        note_ref[at : at + axes, width:] = tile_of(own[:, :width], own[:, width:], *ids)
 
 
 def weigh(axes, own, groups):
-    base = 2 * axes
-    first = own[base + 2 : base + 3, :1]
-    last = own[base + 3 : base + 4, :1]
-    heads = [g[base + 2 : base + 3, :1] for g in groups]
-    tails = [g[base + 3 : base + 4, :1] for g in groups]
+    width = own.shape[1] - LANES
+    half = width + LANES // 2
+    first = own[axes - 1 : axes, width : width + 1]
+    last = own[axes - 1 : axes, half : half + 1]
+    heads = [g[axes - 1 : axes, width : width + 1] for g in groups]
+    tails = [g[axes - 1 : axes, half : half + 1] for g in groups]
     lowest = functools.reduce(jnp.minimum, heads)
     highest = functools.reduce(jnp.maximum, tails)
     weights = []
@@ -147,65 +180,47 @@
     return [tuple(flat[6 * k : 6 * k + 6]) for k in range(count)]
 
 
-def join_own(own_head, own_tail, pairs, weights):
-    head, tail = own_head, own_tail
-    for (group_head, group_tail), w in zip(pairs[1:], weights[1:]):
+def join_own(axes, own, groups, weights):
+    head, tail = own[:axes, :], own[axes:, :]
+    for group, w in zip(groups[1:], weights[1:]):
+        group_head, group_tail = group[:axes, :], group[axes:, :]
         head = head + w[2] * group_head + w[3] * group_tail
         tail = tail + w[4] * group_head + w[5] * group_tail
     return head, tail
 
 
-def join_group(pairs, weights):
-    head = sum(w[0] * pair[0] for pair, w in zip(pairs, weights))
-    tail = sum(w[1] * pair[1] for pair, w in zip(pairs, weights))
+def join_group(axes, groups, weights):
+    head = sum(w[0] * group[:axes, :] for group, w in zip(groups, weights))
+    tail = sum(w[1] * group[axes:, :] for group, w in zip(groups, weights))
     return head, tail
 
 
-def pairs_of(axes, notes):
-    return [(note[:axes, :], note[axes : 2 * axes, :]) for note in notes]
-
-
-def sum_pairs_of(axes, notes):
-    base = 2 * axes
-    return [(note[base : base + 1, :], note[base + 1 : base + 2, :]) for note in notes]
+def mark(ref, axes, first, last):
+    width = ref.shape[1] - LANES
+    left = lax.broadcasted_iota(jnp.int32, (1, LANES), 1) < LANES // 2
+    for row in (axes - 1, 2 * axes - 1):
+        ref[row : row + 1, width:] = jnp.where(left, first, last)
 
 
 def first_join_kernel(axes, count, own_ref, *refs):
     groups = refs[:count]
     own_out, group_out, weight_ref = refs[count:]
+    width = own_ref.shape[1] - LANES
+    half = width + LANES // 2
     weights, lowest, highest = weigh(axes, own_ref, groups)
     store_weights(weight_ref, weights)
-    base = 2 * axes
-    wide = own_ref.shape[1]
-    own_out[base:, :] = own_ref[base:, :]
-    group_out[base:, :] = jnp.zeros((8, wide), F32)
-    group_out[base + 2 : base + 3, :] = jnp.broadcast_to(lowest, (1, wide))
-    group_out[base + 3 : base + 4, :] = jnp.broadcast_to(highest, (1, wide))
-    for pairs, at, size in (
-        (pairs_of(axes, groups), 0, axes),
-        (sum_pairs_of(axes, groups), base, 1),
-    ):
-        head, tail = join_own(
-            own_ref[at : at + size, :], own_ref[at + size : at + 2 * size, :], pairs, weights
-        )
-        own_out[at : at + size, :] = head
-        own_out[at + size : at + 2 * size, :] = tail
-        head, tail = join_group(pairs, weights)
-        group_out[at : at + size, :] = head
-        group_out[at + size : at + 2 * size, :] = tail
+    own_out[:axes, :], own_out[axes:, :] = join_own(axes, own_ref, groups, weights)
+    group_out[:axes, :], group_out[axes:, :] = join_group(axes, groups, weights)
+    mark(own_out, axes, own_ref[axes - 1 : axes, width : width + 1], own_ref[axes - 1 : axes, half : half + 1])
+    mark(group_out, axes, lowest, highest)
 
 
 def join_kernel(axes, count, own_ref, weight_ref, *refs):
     groups = refs[:count]
     own_out, group_out = refs[count:]
     weights = load_weights(weight_ref, count)
-    pairs = pairs_of(axes, groups)
-    head, tail = join_own(own_ref[:axes, :], own_ref[axes:, :], pairs, weights)
-    own_out[:axes, :] = head
-    own_out[axes:, :] = tail
-    head, tail = join_group(pairs, weights)
-    group_out[:axes, :] = head
-    group_out[axes:, :] = tail
+    own_out[:axes, :], own_out[axes:, :] = join_own(axes, own_ref, groups, weights)
+    group_out[:axes, :], group_out[axes:, :] = join_group(axes, groups, weights)
 
 
 def find_frames(axes, columns, centre, live, flat_ref, offset_ref):
@@ -270,36 +285,34 @@
     return lax.broadcasted_iota(jnp.int32, (SLOTS, 1), 0) <= span
 
 
-def second_sweep_kernel(axes, count, points_ref, nodes_ref, part_ref, sums_ref, own_ref, *refs):
+def second_sweep_kernel(axes, count, points_ref, nodes_ref, init_ref, part_ref, sums_ref, own_ref, *refs):
     groups = refs[:count]
-    part_out, note_out, centre_ref, weight_ref, flat_ref, offset_ref, whole_ref, total_ref = refs[count:]
+    part_out, note_out, centre_ref, weight_ref, flat_ref, offset_ref, whole_ref = refs[count:]
     width = points_ref.shape[1]
     first, last = ends_of(nodes_ref)
     span = last - first
     weights, _, _ = weigh(axes, own_ref, groups)
     store_weights(weight_ref, weights)
-    base = 2 * axes
-    head, tail = join_own(
-        own_ref[:axes, :], own_ref[axes:base, :], pairs_of(axes, groups), weights
-    )
+    head, tail = join_own(axes, own_ref, groups, weights)
     flat = SLOTS * axes
     put_rows(whole_ref, part_ref[...], 0, flat)
-    put_rows(whole_ref, tail, pl.multiple_of(span * axes, axes), flat)
-    put_rows(whole_ref, head, 0, flat)
-    head, tail = join_own(
-        own_ref[base : base + 1, :], own_ref[base + 1 : base + 2, :], sum_pairs_of(axes, groups), weights
-    )
-    total_ref[...] = sums_ref[...]
-    total_ref[pl.ds(span, 1), :] = tail
-    total_ref[:1, :] = head
+    put_rows(whole_ref, tail[:, :width], pl.multiple_of(span * axes, axes), flat)
+    put_rows(whole_ref, head[:, :width], 0, flat)
+    counted = width // LANES
+    slots = lax.broadcasted_iota(jnp.int32, (SLOTS, 1), 0)
+    sums = sums_ref[:, :width]
+    counts = sums_ref[:, width:]
+    for slot, tile in ((span, tail[:, width:]), (0, head[:, width:])):
+        sums = jnp.where(slots == slot, sums_of(tile, width), sums)
+        counts = jnp.where(slots == slot, tile[counted : counted + 1], counts)
     live = live_slots(span)
-    counts = jnp.where(live, total_ref[:, width : width + 1], 1.0)
-    centre = total_ref[:, :width] / counts
+    centre = sums / jnp.where(live, counts[:, :1], 1.0)
     centre_ref[...] = centre
+    start = init_ref[...].astype(BF16).astype(F32)
     columns = []
     for index in range(axes):
-        column = get_strided(whole_ref, index, axes)
-        columns.append(column[:, :width] - column[:, width : width + 1] * centre)
+        spread = jnp.sum(sums * start[index : index + 1], 1, keepdims=True)
+        columns.append(get_strided(whole_ref, index, axes) - spread * centre)
     find_frames(axes, columns, centre, live, flat_ref, offset_ref)
     moment, column_sums = sweep_blocks(axes, points_ref, nodes_ref, first, flat_ref, offset_ref)
     emit_part(axes, moment, column_sums, centre_ref[...], span, part_out, note_out)
@@ -309,7 +322,7 @@
     first, last = ends_of(nodes_ref)
     span = last - first
     weights = load_weights(weight_ref, len(groups))
-    head, tail = join_own(own_ref[:axes, :], own_ref[axes:, :], pairs_of(axes, groups), weights)
+    head, tail = join_own(axes, own_ref, groups, weights)
     flat = SLOTS * axes
     put_rows(whole_ref, part_ref[...], 0, flat)
     put_rows(whole_ref, tail, pl.multiple_of(span * axes, axes), flat)
@@ -369,7 +382,8 @@
         pairs = []
         for source in range(devices):
             place = source // stride % radix
-            target = source + ((place + shift) % radix - place) * stride
+            other = place ^ shift if radix & (radix - 1) == 0 else (place + shift) % radix
+            target = source + (other - place) * stride
             pairs.append((source, target))
         groups.append(lax.ppermute(value, ("row", "col"), pairs))
     return groups
@@ -379,14 +393,14 @@
     return jax.ShapeDtypeStruct(dims, F32)
 
 
-def call(kernel, outs, scratch=(), limit=8):
+def call(kernel, outs, scratch=(), limit=8, source=pltpu.VMEM):
     vmem = pl.BlockSpec(memory_space=pltpu.VMEM)
 
     def run(*args):
         return pl.pallas_call(
             kernel,
             out_shape=outs,
-            in_specs=[vmem] * len(args),
+            in_specs=[pl.BlockSpec(memory_space=source)] * len(args),
             out_specs=jax.tree.map(lambda _: vmem, outs),
             scratch_shapes=scratch,
             compiler_params=pltpu.CompilerParams(vmem_limit_bytes=limit * MIB),
@@ -404,15 +418,22 @@
         axes = init_axes.shape[1]
         flat = SLOTS * axes
         wide = width + LANES
-        nodes = node_of_row.reshape(1, rows)
-        note_rows = 2 * axes + 8
         tall = flat * width // LANES
         frame_scratch = [pltpu.VMEM((tall, LANES), F32), pltpu.VMEM((flat, LANES), F32)]
-        part, sums, note = call(
+        part, sums, note, points, nodes, init = call(
             functools.partial(first_sweep_kernel, axes),
-            (shape(flat, wide), shape(SLOTS, wide), shape(note_rows, wide)),
+            (
+                shape(flat, width),
+                shape(SLOTS, wide),
+                shape(2 * axes, wide),
+                jax.ShapeDtypeStruct((rows, width), points.dtype),
+                jax.ShapeDtypeStruct((1, rows), node_of_row.dtype),
+                shape(axes, width),
+            ),
+            [pltpu.SemaphoreType.DMA((len(cuts_of(rows)) + 1,))],
             limit=32,
-        )(points, nodes, init_axes)
+            source=pltpu.HBM,
+        )(*[pltpu.with_memory_space_constraint(each, pltpu.HBM) for each in (points, node_of_row.reshape(1, rows), init_axes.T)])
         own = group = note
         kept = []
         for stage in stages[:-1]:
@@ -420,7 +441,7 @@
             count = len(groups)
             own, group, weight = call(
                 functools.partial(first_join_kernel, axes, count),
-                (shape(note_rows, wide), shape(note_rows, wide), shape(8 * count, LANES)),
+                (shape(2 * axes, wide), shape(2 * axes, wide), shape(8 * count, LANES)),
             )(own, *groups)
             kept.append(weight)
         groups = swap(group, stages[-1], devices)
@@ -428,9 +449,9 @@
         part, note, centre, weight = call(
             functools.partial(second_sweep_kernel, axes, count),
             (shape(flat, width), shape(2 * axes, width), shape(SLOTS, width), shape(8 * count, LANES)),
-            frame_scratch + [pltpu.VMEM((tall + flat, LANES), F32), pltpu.VMEM((SLOTS, wide), F32)],
+            frame_scratch + [pltpu.VMEM((tall, LANES), F32)],
             limit=32,
-        )(points, nodes, part, sums, own, *groups)
+        )(points, nodes, init, part, sums, own, *groups)
         kept.append(weight)
         for repeat in range(1, ITERS):
             own = group = note
@@ -441,18 +462,16 @@
                     (shape(2 * axes, width), shape(2 * axes, width)),
                 )(own, weight, *groups)
             groups = swap(group, stages[-1], devices)
+            settle = frame_scratch + [pltpu.VMEM((tall, LANES), F32)]
             if repeat < ITERS - 1:
                 part, note = call(
                     functools.partial(sweep_kernel, axes, len(groups)),
                     (shape(flat, width), shape(2 * axes, width)),
-                    frame_scratch + [pltpu.VMEM((tall, LANES), F32)],
+                    settle,
                     limit=32,
                 )(points, nodes, part, centre, own, kept[-1], *groups)
         return call(
-            functools.partial(project_kernel, axes, len(groups)),
-            shape(axes, rows),
-            frame_scratch + [pltpu.VMEM((tall, LANES), F32)],
-            limit=32,
+            functools.partial(project_kernel, axes, len(groups)), shape(axes, rows), settle, limit=32
         )(points, nodes, part, centre, own, kept[-1], *groups)
 
     in_specs = (P(("row", "col"), None), P(("row", "col")), P())

time: 89.5 us -> 80.6 us (0.901)
  waiting for transfers between devices: 34.3 us -> 26.8 us
  local copies, waits for them, and re-layouts: 6.22 us -> 0 us
  starting transfers between devices: 22.4 us -> 25.6 us
  Pallas kernels: 26.3 us -> 27.8 us
    ppermute x21, waiting for transfers between devices: 34.3 us -> 26.8 us  [swap(): groups.append(lax.ppermute(value, ('row', 'col'), pairs))]
    unnamed x5 -> x0, local copies, waits for them, and re-layouts: 6.22 us -> none
    ppermute x21, starting transfers between devices: 22.4 us -> 25.6 us  [swap(): groups.append(lax.ppermute(value, ('row', 'col'), pairs))]
    pallas_call x10, Pallas kernels: 26.3 us -> 27.8 us  [run(): pl.pallas_call(kernel, out_shape=outs, in_specs=[pl.BlockSpec(memory_spac...]
  transfers between devices with their start and end apart: 21 -> 21, of which waited for: 19 -> 15; matrix products, arithmetic and copies ran while one was open for 0% -> 0% of each run, Pallas kernels for 0% -> 0%
where the time goes in v2:
time: 80.6 us; the launch traced here: 80.4 us
  Pallas kernels  27.8 us (34%)
  waiting for transfers between devices  26.8 us (33%)
  starting transfers between devices  25.6 us (32%)
    pallas_call x10, Pallas kernels, run(): pl.pallas_call(kernel, out_shape=outs, in_specs=[pl.BlockSpec(memory_spac...  27.8 us
    ppermute x21, waiting for transfers between devices, swap(): groups.append(lax.ppermute(value, ('row', 'col'), pairs))  26.8 us
    ppermute x21, starting transfers between devices, swap(): groups.append(lax.ppermute(value, ('row', 'col'), pairs))  25.6 us
  transfers between devices with their start and end apart: 21, of which 15 were waited for; matrix products, arithmetic and copies ran while one was open for 0% of the time, Pallas kernels for 0%

profile of v2, /device:TPU:0, one launch (start us, length us, event | category | flops | bytes accessed | tf_op | source)
XLA Modules:
  0.0 80.4 jit_solution(16428348680236525693)
XLA Ops:
  0.0 8.0 %shard_map.37 = (f32[64,768]{1,0:T(8,128)S(1)}, f32[8,896]{1,0:T(8,128)S(1)}, f32[16,896]{1,0:T(8,128)S(1)}, bf16[8192,768]{1,0:T(8,128)(2,1)S(1)}, s32[1,8192]{1,0:T(1,128)S(1)}, /*index=5*/f32[8,768]{1,0:T(8,128)S(1)}) custom-call(bf16[8192,768]{1,0:T(8,128)(2,1)} %points_hbm.1, s32[1,8192]{1,0:T(1,128)} %bitcast.2, f32[8,768]{1,0:T(8,128)} %bitcast.3), custom_call_target="tpu_custom_call" | custom-call | tf_op jit(solution)/shard_map/pallas_call | solution.py:400
  8.0 3.0 %collective-permute-start = (f32[16,896]{1,0:T(8,128)S(1)}, f32[16,896]{1,0:T(8,128)S(1)}, u32[]{:S(2)}, u32[]{:S(2)}) collective-permute-start(f32[16,896]{1,0:T(8,128)S(1)} %get-tuple-element.36.own_ref.refs_0_), channel_id=1, source_target_pairs={{0,1},{1,0},{2,3},{3,2},{4,5},{5,4},{6,7},{7,6},{8,9},{9,8},{10,11... | collective-permute-start | bytes 172040 | tf_op jit(solution)/shard_map/ppermute | solution.py:388
  11.0 2.2 %collective-permute-done.refs_1_ = f32[16,896]{1,0:T(8,128)S(1)} collective-permute-done((f32[16,896]{1,0:T(8,128)S(1)}, f32[16,896]{1,0:T(8,128)S(1)}, u32[]{:S(2)}, u32[]{:S(2)}) %collective-permute-start) | collective-permute-done | bytes 57376 | tf_op jit(solution)/shard_map/ppermute | solution.py:388
  13.2 0.2 shard_map.38
  13.4 4.2 %collective-permute-start.3 = (f32[16,896]{1,0:T(8,128)S(1)}, f32[16,896]{1,0:T(8,128)S(1)}, u32[]{:S(2)}, u32[]{:S(2)}) collective-permute-start(f32[16,896]{1,0:T(8,128)S(1)} %get-tuple-element.38.refs_0_), channel_id=1, source_target_pairs={{0,6},{1,7},{2,4},{3,5},{4,2},{5,3},{6,0},{7,1},{8,14},{9,15},{10,... | collective-permute-start | bytes 172040 | tf_op jit(solution)/shard_map/ppermute | solution.py:388
  17.6 0.6 collective-permute-start.1
  18.3 1.6 %collective-permute-done.3.refs_3_ = f32[16,896]{1,0:T(8,128)S(1)} collective-permute-done((f32[16,896]{1,0:T(8,128)S(1)}, f32[16,896]{1,0:T(8,128)S(1)}, u32[]{:S(2)}, u32[]{:S(2)}) %collective-permute-start.3) | collective-permute-done | bytes 57376 | tf_op jit(solution)/shard_map/ppermute | solution.py:388
  19.9 2.8 %collective-permute-done.2.refs_2_ = f32[16,896]{1,0:T(8,128)S(1)} collective-permute-done((f32[16,896]{1,0:T(8,128)S(1)}, f32[16,896]{1,0:T(8,128)S(1)}, u32[]{:S(2)}, u32[]{:S(2)}) %collective-permute-start.2) | collective-permute-done | bytes 57376 | tf_op jit(solution)/shard_map/ppermute | solution.py:388
  22.7 0.0 collective-permute-done.1.refs_1_
  22.7 0.3 shard_map.39
  23.0 0.1 collective-permute-start.6
  23.1 1.6 %collective-permute-start.5 = (f32[16,896]{1,0:T(8,128)S(1)}, f32[16,896]{1,0:T(8,128)S(1)}, u32[]{:S(2)}, u32[]{:S(2)}) collective-permute-start(f32[16,896]{1,0:T(8,128)S(1)} %get-tuple-element.40.refs_0_), channel_id=1, source_target_pairs={{0,16},{1,17},{2,18},{3,19},{4,20},{5,21},{6,22},{7,23},{8,24},{9,... | collective-permute-start | bytes 172040 | tf_op jit(solution)/shard_map/ppermute | solution.py:388
  24.7 0.2 collective-permute-start.4
  24.9 2.3 %collective-permute-done.6.refs_3_ = f32[16,896]{1,0:T(8,128)S(1)} collective-permute-done((f32[16,896]{1,0:T(8,128)S(1)}, f32[16,896]{1,0:T(8,128)S(1)}, u32[]{:S(2)}, u32[]{:S(2)}) %collective-permute-start.6) | collective-permute-done | bytes 57376 | tf_op jit(solution)/shard_map/ppermute | solution.py:388
  27.2 1.3 %collective-permute-done.5.refs_2_ = f32[16,896]{1,0:T(8,128)S(1)} collective-permute-done((f32[16,896]{1,0:T(8,128)S(1)}, f32[16,896]{1,0:T(8,128)S(1)}, u32[]{:S(2)}, u32[]{:S(2)}) %collective-permute-start.5) | collective-permute-done | bytes 57376 | tf_op jit(solution)/shard_map/ppermute | solution.py:388
  28.5 0.0 collective-permute-done.4.refs_1_
  28.5 6.7 %shard_map.40 = (f32[64,768]{1,0:T(8,128)S(1)}, f32[16,768]{1,0:T(8,128)S(1)}, f32[8,768]{1,0:T(8,128)S(1)}, f32[32,128]{1,0:T(8,128)S(1)}) custom-call(bf16[8192,768]{1,0:T(8,128)(2,1)S(1)} %get-tuple-element.31.points_ref, s32[1,8192]{1,0:T(1,128)S(1)} %get-tuple-element.32.nodes_ref, f32[8,768]{1,0:T(8,128)S(1)} %get-tuple-element.33.init_ref, ...), custom_call_target="tpu_custom_call" | custom-call | tf_op jit(solution)/shard_map/pallas_call | solution.py:400
  35.2 1.6 %collective-permute-start.7 = (f32[16,768]{1,0:T(8,128)S(1)}, f32[16,768]{1,0:T(8,128)S(1)}, u32[]{:S(2)}, u32[]{:S(2)}) collective-permute-start(f32[16,768]{1,0:T(8,128)S(1)} %get-tuple-element.43.own_ref.refs_0_), channel_id=1, source_target_pairs={{0,1},{1,0},{2,3},{3,2},{4,5},{5,4},{6,7},{7,6},{8,9},{9,8},{10,11... | collective-permute-start | bytes 147464 | tf_op jit(solution)/shard_map/ppermute | solution.py:388
  36.8 2.6 %collective-permute-done.7.refs_1_ = f32[16,768]{1,0:T(8,128)S(1)} collective-permute-done((f32[16,768]{1,0:T(8,128)S(1)}, f32[16,768]{1,0:T(8,128)S(1)}, u32[]{:S(2)}, u32[]{:S(2)}) %collective-permute-start.7) | collective-permute-done | bytes 49184 | tf_op jit(solution)/shard_map/ppermute | solution.py:388
  39.3 0.1 shard_map.41
  39.4 1.8 %collective-permute-start.10 = (f32[16,768]{1,0:T(8,128)S(1)}, f32[16,768]{1,0:T(8,128)S(1)}, u32[]{:S(2)}, u32[]{:S(2)}) collective-permute-start(f32[16,768]{1,0:T(8,128)S(1)} %get-tuple-element.47.refs_0_), channel_id=1, source_target_pairs={{0,6},{1,7},{2,4},{3,5},{4,2},{5,3},{6,0},{7,1},{8,14},{9,15},{10,... | collective-permute-start | bytes 147464 | tf_op jit(solution)/shard_map/ppermute | solution.py:388
  41.2 0.4 collective-permute-start.9
  41.6 2.3 %collective-permute-start.8 = (f32[16,768]{1,0:T(8,128)S(1)}, f32[16,768]{1,0:T(8,128)S(1)}, u32[]{:S(2)}, u32[]{:S(2)}) collective-permute-start(f32[16,768]{1,0:T(8,128)S(1)} %get-tuple-element.47.refs_0_), channel_id=1, source_target_pairs={{0,2},{1,3},{2,0},{3,1},{4,6},{5,7},{6,4},{7,5},{8,10},{9,11},{10,... | collective-permute-start | bytes 147464 | tf_op jit(solution)/shard_map/ppermute | solution.py:388
  43.9 1.7 %collective-permute-done.10.refs_3_ = f32[16,768]{1,0:T(8,128)S(1)} collective-permute-done((f32[16,768]{1,0:T(8,128)S(1)}, f32[16,768]{1,0:T(8,128)S(1)}, u32[]{:S(2)}, u32[]{:S(2)}) %collective-permute-start.10) | collective-permute-done | bytes 49184 | tf_op jit(solution)/shard_map/ppermute | solution.py:388
  45.6 1.1 %collective-permute-done.9.refs_2_ = f32[16,768]{1,0:T(8,128)S(1)} collective-permute-done((f32[16,768]{1,0:T(8,128)S(1)}, f32[16,768]{1,0:T(8,128)S(1)}, u32[]{:S(2)}, u32[]{:S(2)}) %collective-permute-start.9) | collective-permute-done | bytes 49184 | tf_op jit(solution)/shard_map/ppermute | solution.py:388
  46.7 0.1 shard_map.42
  46.8 0.1 collective-permute-start.13
  46.8 1.0 %collective-permute-start.12 = (f32[16,768]{1,0:T(8,128)S(1)}, f32[16,768]{1,0:T(8,128)S(1)}, u32[]{:S(2)}, u32[]{:S(2)}) collective-permute-start(f32[16,768]{1,0:T(8,128)S(1)} %get-tuple-element.50.refs_0_), channel_id=1, source_target_pairs={{0,16},{1,17},{2,18},{3,19},{4,20},{5,21},{6,22},{7,23},{8,24},{9,... | collective-permute-start | bytes 147464 | tf_op jit(solution)/shard_map/ppermute | solution.py:388
  47.8 0.9 %collective-permute-start.11 = (f32[16,768]{1,0:T(8,128)S(1)}, f32[16,768]{1,0:T(8,128)S(1)}, u32[]{:S(2)}, u32[]{:S(2)}) collective-permute-start(f32[16,768]{1,0:T(8,128)S(1)} %get-tuple-element.50.refs_0_), channel_id=1, source_target_pairs={{0,8},{1,9},{2,10},{3,11},{4,12},{5,13},{6,14},{7,15},{8,0},{9,1},... | collective-permute-start | bytes 147464 | tf_op jit(solution)/shard_map/ppermute | solution.py:388
  48.7 1.7 %collective-permute-done.13.refs_3_ = f32[16,768]{1,0:T(8,128)S(1)} collective-permute-done((f32[16,768]{1,0:T(8,128)S(1)}, f32[16,768]{1,0:T(8,128)S(1)}, u32[]{:S(2)}, u32[]{:S(2)}) %collective-permute-start.13) | collective-permute-done | bytes 49184 | tf_op jit(solution)/shard_map/ppermute | solution.py:388
  50.4 1.2 %collective-permute-done.12.refs_2_ = f32[16,768]{1,0:T(8,128)S(1)} collective-permute-done((f32[16,768]{1,0:T(8,128)S(1)}, f32[16,768]{1,0:T(8,128)S(1)}, u32[]{:S(2)}, u32[]{:S(2)}) %collective-permute-start.12) | collective-permute-done | bytes 49184 | tf_op jit(solution)/shard_map/ppermute | solution.py:388
  51.5 6.8 %shard_map.43 = (f32[64,768]{1,0:T(8,128)S(1)}, f32[16,768]{1,0:T(8,128)S(1)}) custom-call(bf16[8192,768]{1,0:T(8,128)(2,1)S(1)} %get-tuple-element.31.points_ref, s32[1,8192]{1,0:T(1,128)S(1)} %get-tuple-element.32.nodes_ref, f32[64,768]{1,0:T(8,128)S(1)} %get-tuple-element.41.part_ref, f32[8,768]{1,0:T(8,128)S(1)} %get-tuple-element.42.centre_ref, ...), custom_call_target="tpu_custom_call" | custom-call | tf_op jit(solution)/shard_map/pallas_call | solution.py:400
  58.3 1.6 %collective-permute-start.14 = (f32[16,768]{1,0:T(8,128)S(1)}, f32[16,768]{1,0:T(8,128)S(1)}, u32[]{:S(2)}, u32[]{:S(2)}) collective-permute-start(f32[16,768]{1,0:T(8,128)S(1)} %get-tuple-element.52.own_ref.refs_0_), channel_id=1, source_target_pairs={{0,1},{1,0},{2,3},{3,2},{4,5},{5,4},{6,7},{7,6},{8,9},{9,8},{10,11... | collective-permute-start | bytes 147464 | tf_op jit(solution)/shard_map/ppermute | solution.py:388
  59.9 2.6 %collective-permute-done.14.refs_1_ = f32[16,768]{1,0:T(8,128)S(1)} collective-permute-done((f32[16,768]{1,0:T(8,128)S(1)}, f32[16,768]{1,0:T(8,128)S(1)}, u32[]{:S(2)}, u32[]{:S(2)}) %collective-permute-start.14) | collective-permute-done | bytes 49184 | tf_op jit(solution)/shard_map/ppermute | solution.py:388
  62.5 2.4 %collective-permute-start.17 = (f32[16,768]{1,0:T(8,128)S(1)}, f32[16,768]{1,0:T(8,128)S(1)}, u32[]{:S(2)}, u32[]{:S(2)}) collective-permute-start(f32[16,768]{1,0:T(8,128)S(1)} %get-tuple-element.54.refs_0_), channel_id=1, source_target_pairs={{0,6},{1,7},{2,4},{3,5},{4,2},{5,3},{6,0},{7,1},{8,14},{9,15},{10,... | collective-permute-start | bytes 147464 | tf_op jit(solution)/shard_map/ppermute | solution.py:388
  64.9 0.4 collective-permute-start.16
  65.3 1.7 %collective-permute-start.15 = (f32[16,768]{1,0:T(8,128)S(1)}, f32[16,768]{1,0:T(8,128)S(1)}, u32[]{:S(2)}, u32[]{:S(2)}) collective-permute-start(f32[16,768]{1,0:T(8,128)S(1)} %get-tuple-element.54.refs_0_), channel_id=1, source_target_pairs={{0,2},{1,3},{2,0},{3,1},{4,6},{5,7},{6,4},{7,5},{8,10},{9,11},{10,... | collective-permute-start | bytes 147464 | tf_op jit(solution)/shard_map/ppermute | solution.py:388
  67.0 1.7 %collective-permute-done.17.refs_3_ = f32[16,768]{1,0:T(8,128)S(1)} collective-permute-done((f32[16,768]{1,0:T(8,128)S(1)}, f32[16,768]{1,0:T(8,128)S(1)}, u32[]{:S(2)}, u32[]{:S(2)}) %collective-permute-start.17) | collective-permute-done | bytes 49184 | tf_op jit(solution)/shard_map/ppermute | solution.py:388
  68.7 1.4 %collective-permute-done.16.refs_2_ = f32[16,768]{1,0:T(8,128)S(1)} collective-permute-done((f32[16,768]{1,0:T(8,128)S(1)}, f32[16,768]{1,0:T(8,128)S(1)}, u32[]{:S(2)}, u32[]{:S(2)}) %collective-permute-start.16) | collective-permute-done | bytes 49184 | tf_op jit(solution)/shard_map/ppermute | solution.py:388
  70.1 0.0 collective-permute-done.15.refs_1_
  70.1 0.1 shard_map.45
  70.1 0.1 collective-permute-start.20
  70.2 0.9 %collective-permute-start.19 = (f32[16,768]{1,0:T(8,128)S(1)}, f32[16,768]{1,0:T(8,128)S(1)}, u32[]{:S(2)}, u32[]{:S(2)}) collective-permute-start(f32[16,768]{1,0:T(8,128)S(1)} %get-tuple-element.56.refs_0_), channel_id=1, source_target_pairs={{0,16},{1,17},{2,18},{3,19},{4,20},{5,21},{6,22},{7,23},{8,24},{9,... | collective-permute-start | bytes 147464 | tf_op jit(solution)/shard_map/ppermute | solution.py:388
  71.2 0.9 %collective-permute-start.18 = (f32[16,768]{1,0:T(8,128)S(1)}, f32[16,768]{1,0:T(8,128)S(1)}, u32[]{:S(2)}, u32[]{:S(2)}) collective-permute-start(f32[16,768]{1,0:T(8,128)S(1)} %get-tuple-element.56.refs_0_), channel_id=1, source_target_pairs={{0,8},{1,9},{2,10},{3,11},{4,12},{5,13},{6,14},{7,15},{8,0},{9,1},... | collective-permute-start | bytes 147464 | tf_op jit(solution)/shard_map/ppermute | solution.py:388
  72.1 1.7 %collective-permute-done.20.refs_3_ = f32[16,768]{1,0:T(8,128)S(1)} collective-permute-done((f32[16,768]{1,0:T(8,128)S(1)}, f32[16,768]{1,0:T(8,128)S(1)}, u32[]{:S(2)}, u32[]{:S(2)}) %collective-permute-start.20) | collective-permute-done | bytes 49184 | tf_op jit(solution)/shard_map/ppermute | solution.py:388
  73.7 1.1 %collective-permute-done.19.refs_2_ = f32[16,768]{1,0:T(8,128)S(1)} collective-permute-done((f32[16,768]{1,0:T(8,128)S(1)}, f32[16,768]{1,0:T(8,128)S(1)}, u32[]{:S(2)}, u32[]{:S(2)}) %collective-permute-start.19) | collective-permute-done | bytes 49184 | tf_op jit(solution)/shard_map/ppermute | solution.py:388
  74.8 0.0 collective-permute-done.18.refs_1_
  74.8 5.6 %shard_map.46 = f32[8,8192]{1,0:T(8,128)} custom-call(bf16[8192,768]{1,0:T(8,128)(2,1)S(1)} %get-tuple-element.31.points_ref, s32[1,8192]{1,0:T(1,128)S(1)} %get-tuple-element.32.nodes_ref, f32[64,768]{1,0:T(8,128)S(1)} %get-tuple-element.51.part_ref, f32[8,768]{1,0:T(8,128)S(1)} %get-tuple-element.42.centre_ref, f32[16,768]{1,0:T(8,128)S(1)} %get-tuple-element.55.own_ref, ...), custom_call_target="tpu_custom_call" | custom-call | tf_op jit(solution)/shard_map/pallas_call | solution.py:400
  (4 shorter events, 0.1 us)
Async XLA Ops:
  8.0 5.1 %collective-permute-start = (f32[16,896]{1,0:T(8,128)S(1)}, f32[16,896]{1,0:T(8,128)S(1)}, u32[]{:S(2)}, u32[]{:S(2)}) collective-permute-start(f32[16,896]{1,0:T(8,128)S(1)} %get-tuple-element.36.own_ref.refs_0_), channel_id=1, source_target_pairs={{0,1},{1,0},{2,3},{3,2},{4,5},{5,4},{6,7},{7,6},{8,9},{9,8},{10,11... | collective-permute-start | bytes 172040 | tf_op jit(solution)/shard_map/ppermute | solution.py:388
  13.4 6.4 %collective-permute-start.3 = (f32[16,896]{1,0:T(8,128)S(1)}, f32[16,896]{1,0:T(8,128)S(1)}, u32[]{:S(2)}, u32[]{:S(2)}) collective-permute-start(f32[16,896]{1,0:T(8,128)S(1)} %get-tuple-element.38.refs_0_), channel_id=1, source_target_pairs={{0,6},{1,7},{2,4},{3,5},{4,2},{5,3},{6,0},{7,1},{8,14},{9,15},{10,... | collective-permute-start | bytes 172040 | tf_op jit(solution)/shard_map/ppermute | solution.py:388
  17.6 5.1 %collective-permute-start.2 = (f32[16,896]{1,0:T(8,128)S(1)}, f32[16,896]{1,0:T(8,128)S(1)}, u32[]{:S(2)}, u32[]{:S(2)}) collective-permute-start(f32[16,896]{1,0:T(8,128)S(1)} %get-tuple-element.38.refs_0_), channel_id=1, source_target_pairs={{0,4},{1,5},{2,6},{3,7},{4,0},{5,1},{6,2},{7,3},{8,12},{9,13},{10,... | collective-permute-start | bytes 172040 | tf_op jit(solution)/shard_map/ppermute | solution.py:388
  17.6 5.1 %collective-permute-start.1 = (f32[16,896]{1,0:T(8,128)S(1)}, f32[16,896]{1,0:T(8,128)S(1)}, u32[]{:S(2)}, u32[]{:S(2)}) collective-permute-start(f32[16,896]{1,0:T(8,128)S(1)} %get-tuple-element.38.refs_0_), channel_id=1, source_target_pairs={{0,2},{1,3},{2,0},{3,1},{4,6},{5,7},{6,4},{7,5},{8,10},{9,11},{10,... | collective-permute-start | bytes 172040 | tf_op jit(solution)/shard_map/ppermute | solution.py:388
  23.0 4.2 %collective-permute-start.6 = (f32[16,896]{1,0:T(8,128)S(1)}, f32[16,896]{1,0:T(8,128)S(1)}, u32[]{:S(2)}, u32[]{:S(2)}) collective-permute-start(f32[16,896]{1,0:T(8,128)S(1)} %get-tuple-element.40.refs_0_), channel_id=1, source_target_pairs={{0,24},{1,25},{2,26},{3,27},{4,28},{5,29},{6,30},{7,31},{8,16},{9,... | collective-permute-start | bytes 172040 | tf_op jit(solution)/shard_map/ppermute | solution.py:388
  23.1 5.4 %collective-permute-start.5 = (f32[16,896]{1,0:T(8,128)S(1)}, f32[16,896]{1,0:T(8,128)S(1)}, u32[]{:S(2)}, u32[]{:S(2)}) collective-permute-start(f32[16,896]{1,0:T(8,128)S(1)} %get-tuple-element.40.refs_0_), channel_id=1, source_target_pairs={{0,16},{1,17},{2,18},{3,19},{4,20},{5,21},{6,22},{7,23},{8,24},{9,... | collective-permute-start | bytes 172040 | tf_op jit(solution)/shard_map/ppermute | solution.py:388
  24.7 3.8 %collective-permute-start.4 = (f32[16,896]{1,0:T(8,128)S(1)}, f32[16,896]{1,0:T(8,128)S(1)}, u32[]{:S(2)}, u32[]{:S(2)}) collective-permute-start(f32[16,896]{1,0:T(8,128)S(1)} %get-tuple-element.40.refs_0_), channel_id=1, source_target_pairs={{0,8},{1,9},{2,10},{3,11},{4,12},{5,13},{6,14},{7,15},{8,0},{9,1},... | collective-permute-start | bytes 172040 | tf_op jit(solution)/shard_map/ppermute | solution.py:388
  35.2 4.2 %collective-permute-start.7 = (f32[16,768]{1,0:T(8,128)S(1)}, f32[16,768]{1,0:T(8,128)S(1)}, u32[]{:S(2)}, u32[]{:S(2)}) collective-permute-start(f32[16,768]{1,0:T(8,128)S(1)} %get-tuple-element.43.own_ref.refs_0_), channel_id=1, source_target_pairs={{0,1},{1,0},{2,3},{3,2},{4,5},{5,4},{6,7},{7,6},{8,9},{9,8},{10,11... | collective-permute-start | bytes 147464 | tf_op jit(solution)/shard_map/ppermute | solution.py:388
  39.4 6.2 %collective-permute-start.10 = (f32[16,768]{1,0:T(8,128)S(1)}, f32[16,768]{1,0:T(8,128)S(1)}, u32[]{:S(2)}, u32[]{:S(2)}) collective-permute-start(f32[16,768]{1,0:T(8,128)S(1)} %get-tuple-element.47.refs_0_), channel_id=1, source_target_pairs={{0,6},{1,7},{2,4},{3,5},{4,2},{5,3},{6,0},{7,1},{8,14},{9,15},{10,... | collective-permute-start | bytes 147464 | tf_op jit(solution)/shard_map/ppermute | solution.py:388
  41.2 5.5 %collective-permute-start.9 = (f32[16,768]{1,0:T(8,128)S(1)}, f32[16,768]{1,0:T(8,128)S(1)}, u32[]{:S(2)}, u32[]{:S(2)}) collective-permute-start(f32[16,768]{1,0:T(8,128)S(1)} %get-tuple-element.47.refs_0_), channel_id=1, source_target_pairs={{0,4},{1,5},{2,6},{3,7},{4,0},{5,1},{6,2},{7,3},{8,12},{9,13},{10,... | collective-permute-start | bytes 147464 | tf_op jit(solution)/shard_map/ppermute | solution.py:388
  41.6 5.1 %collective-permute-start.8 = (f32[16,768]{1,0:T(8,128)S(1)}, f32[16,768]{1,0:T(8,128)S(1)}, u32[]{:S(2)}, u32[]{:S(2)}) collective-permute-start(f32[16,768]{1,0:T(8,128)S(1)} %get-tuple-element.47.refs_0_), channel_id=1, source_target_pairs={{0,2},{1,3},{2,0},{3,1},{4,6},{5,7},{6,4},{7,5},{8,10},{9,11},{10,... | collective-permute-start | bytes 147464 | tf_op jit(solution)/shard_map/ppermute | solution.py:388
  46.8 3.6 %collective-permute-start.13 = (f32[16,768]{1,0:T(8,128)S(1)}, f32[16,768]{1,0:T(8,128)S(1)}, u32[]{:S(2)}, u32[]{:S(2)}) collective-permute-start(f32[16,768]{1,0:T(8,128)S(1)} %get-tuple-element.50.refs_0_), channel_id=1, source_target_pairs={{0,24},{1,25},{2,26},{3,27},{4,28},{5,29},{6,30},{7,31},{8,16},{9,... | collective-permute-start | bytes 147464 | tf_op jit(solution)/shard_map/ppermute | solution.py:388
  46.8 4.7 %collective-permute-start.12 = (f32[16,768]{1,0:T(8,128)S(1)}, f32[16,768]{1,0:T(8,128)S(1)}, u32[]{:S(2)}, u32[]{:S(2)}) collective-permute-start(f32[16,768]{1,0:T(8,128)S(1)} %get-tuple-element.50.refs_0_), channel_id=1, source_target_pairs={{0,16},{1,17},{2,18},{3,19},{4,20},{5,21},{6,22},{7,23},{8,24},{9,... | collective-permute-start | bytes 147464 | tf_op jit(solution)/shard_map/ppermute | solution.py:388
  47.8 3.7 %collective-permute-start.11 = (f32[16,768]{1,0:T(8,128)S(1)}, f32[16,768]{1,0:T(8,128)S(1)}, u32[]{:S(2)}, u32[]{:S(2)}) collective-permute-start(f32[16,768]{1,0:T(8,128)S(1)} %get-tuple-element.50.refs_0_), channel_id=1, source_target_pairs={{0,8},{1,9},{2,10},{3,11},{4,12},{5,13},{6,14},{7,15},{8,0},{9,1},... | collective-permute-start | bytes 147464 | tf_op jit(solution)/shard_map/ppermute | solution.py:388
  58.3 4.2 %collective-permute-start.14 = (f32[16,768]{1,0:T(8,128)S(1)}, f32[16,768]{1,0:T(8,128)S(1)}, u32[]{:S(2)}, u32[]{:S(2)}) collective-permute-start(f32[16,768]{1,0:T(8,128)S(1)} %get-tuple-element.52.own_ref.refs_0_), channel_id=1, source_target_pairs={{0,1},{1,0},{2,3},{3,2},{4,5},{5,4},{6,7},{7,6},{8,9},{9,8},{10,11... | collective-permute-start | bytes 147464 | tf_op jit(solution)/shard_map/ppermute | solution.py:388
  62.5 6.2 %collective-permute-start.17 = (f32[16,768]{1,0:T(8,128)S(1)}, f32[16,768]{1,0:T(8,128)S(1)}, u32[]{:S(2)}, u32[]{:S(2)}) collective-permute-start(f32[16,768]{1,0:T(8,128)S(1)} %get-tuple-element.54.refs_0_), channel_id=1, source_target_pairs={{0,6},{1,7},{2,4},{3,5},{4,2},{5,3},{6,0},{7,1},{8,14},{9,15},{10,... | collective-permute-start | bytes 147464 | tf_op jit(solution)/shard_map/ppermute | solution.py:388
  64.9 5.2 %collective-permute-start.16 = (f32[16,768]{1,0:T(8,128)S(1)}, f32[16,768]{1,0:T(8,128)S(1)}, u32[]{:S(2)}, u32[]{:S(2)}) collective-permute-start(f32[16,768]{1,0:T(8,128)S(1)} %get-tuple-element.54.refs_0_), channel_id=1, source_target_pairs={{0,4},{1,5},{2,6},{3,7},{4,0},{5,1},{6,2},{7,3},{8,12},{9,13},{10,... | collective-permute-start | bytes 147464 | tf_op jit(solution)/shard_map/ppermute | solution.py:388
  65.3 4.8 %collective-permute-start.15 = (f32[16,768]{1,0:T(8,128)S(1)}, f32[16,768]{1,0:T(8,128)S(1)}, u32[]{:S(2)}, u32[]{:S(2)}) collective-permute-start(f32[16,768]{1,0:T(8,128)S(1)} %get-tuple-element.54.refs_0_), channel_id=1, source_target_pairs={{0,2},{1,3},{2,0},{3,1},{4,6},{5,7},{6,4},{7,5},{8,10},{9,11},{10,... | collective-permute-start | bytes 147464 | tf_op jit(solution)/shard_map/ppermute | solution.py:388
  70.1 3.6 %collective-permute-start.20 = (f32[16,768]{1,0:T(8,128)S(1)}, f32[16,768]{1,0:T(8,128)S(1)}, u32[]{:S(2)}, u32[]{:S(2)}) collective-permute-start(f32[16,768]{1,0:T(8,128)S(1)} %get-tuple-element.56.refs_0_), channel_id=1, source_target_pairs={{0,24},{1,25},{2,26},{3,27},{4,28},{5,29},{6,30},{7,31},{8,16},{9,... | collective-permute-start | bytes 147464 | tf_op jit(solution)/shard_map/ppermute | solution.py:388
  70.2 4.6 %collective-permute-start.19 = (f32[16,768]{1,0:T(8,128)S(1)}, f32[16,768]{1,0:T(8,128)S(1)}, u32[]{:S(2)}, u32[]{:S(2)}) collective-permute-start(f32[16,768]{1,0:T(8,128)S(1)} %get-tuple-element.56.refs_0_), channel_id=1, source_target_pairs={{0,16},{1,17},{2,18},{3,19},{4,20},{5,21},{6,22},{7,23},{8,24},{9,... | collective-permute-start | bytes 147464 | tf_op jit(solution)/shard_map/ppermute | solution.py:388
  71.2 3.7 %collective-permute-start.18 = (f32[16,768]{1,0:T(8,128)S(1)}, f32[16,768]{1,0:T(8,128)S(1)}, u32[]{:S(2)}, u32[]{:S(2)}) collective-permute-start(f32[16,768]{1,0:T(8,128)S(1)} %get-tuple-element.56.refs_0_), channel_id=1, source_target_pairs={{0,8},{1,9},{2,10},{3,11},{4,12},{5,13},{6,14},{7,15},{8,0},{9,1},... | collective-permute-start | bytes 147464 | tf_op jit(solution)/shard_map/ppermute | solution.py:388

commit v3 on v2

--- a/solution.py
+++ b/solution.py
@@ -10,10 +10,10 @@
 ITERS = 3
 SLOTS = 8
 LANES = 128
-BLOCK = 2048
-PIECE = 1024
+BLOCK = 512
+PIECE = 512
 AHEAD = 3
-FIRST = 1024
+FIRST = 2048
 STEP = 2048
 F32 = jnp.float32
 BF16 = jnp.bfloat16
@@ -105,7 +105,6 @@
     first, last = ends_of(nodes_ref)
     frame = init_ref[...].astype(BF16)
     slot_rows = SLOTS * axes
-    moment = jnp.zeros((2 * slot_rows + SLOTS, width), F32)
     counts = jnp.zeros((SLOTS, LANES), F32)
     left = block = None
     for start in range(0, rows, PIECE):
@@ -118,7 +117,9 @@
         block = points_ref[start : start + PIECE, :]
         spread = dot_nt(frame, block)
         if start > 0:
-            moment = moment + dot_nn(left_before, before)
+            product = dot_nn(left_before, before)
+            part_ref[...] = product[:slot_rows] + product[slot_rows : 2 * slot_rows] + (part_ref[...] if start > PIECE else 0.0)
+            sums_ref[:, :width] = product[2 * slot_rows :] + (sums_ref[:, :width] if start > PIECE else 0.0)
         slot_of = nodes_ref[:, start : start + PIECE] - first
         high = spread.astype(BF16).astype(F32)
         low = spread - high
@@ -131,9 +132,9 @@
         member = (slot_of == lax.broadcasted_iota(jnp.int32, (SLOTS, PIECE), 0)).astype(F32)
         left = jnp.concatenate(highs + lows + [member], 0).astype(BF16)
         counts = counts + fold_lanes(member)
-    moment = moment + dot_nn(left, block)
-    part_ref[...] = moment[:slot_rows] + moment[slot_rows : 2 * slot_rows]
-    sums_ref[:, :width] = moment[2 * slot_rows :]
+    product = dot_nn(left, block)
+    part_ref[...] += product[:slot_rows] + product[slot_rows : 2 * slot_rows]
+    sums_ref[:, :width] += product[2 * slot_rows :]
     sums_ref[:, width:] = jnp.broadcast_to(jnp.sum(counts, 1, keepdims=True), counts.shape)
     span = last - first
     ids = (first.astype(F32), last.astype(F32))
@@ -175,9 +176,9 @@
         weight_ref[index : index + 1, :] = jnp.broadcast_to(weight, (1, LANES))
 
 
-def load_weights(weight_ref, count):
-    flat = [weight_ref[index : index + 1, :1] for index in range(6 * count)]
-    return [tuple(flat[6 * k : 6 * k + 6]) for k in range(count)]
+def load_weights(weight_ref, count, kinds=6):
+    flat = [weight_ref[index : index + 1, :1] for index in range(kinds * count)]
+    return [tuple(flat[kinds * k : kinds * (k + 1)]) for k in range(count)]
 
 
 def join_own(axes, own, groups, weights):
@@ -198,29 +199,83 @@
 def mark(ref, axes, first, last):
     width = ref.shape[1] - LANES
     left = lax.broadcasted_iota(jnp.int32, (1, LANES), 1) < LANES // 2
-    for row in (axes - 1, 2 * axes - 1):
+    for row in range(axes - 1, ref.shape[0], axes):
         ref[row : row + 1, width:] = jnp.where(left, first, last)
 
 
-def first_join_kernel(axes, count, own_ref, *refs):
+def place_of(stage):
+    stride, radix = stage
+    index = lax.axis_index("row") * lax.axis_size("col") + lax.axis_index("col")
+    return index // stride % radix
+
+
+def partner(place, shift, radix):
+    return place ^ shift if radix & (radix - 1) == 0 else (place + shift) % radix
+
+
+def put_sends(sends, stage, head, tail):
+    place = place_of(stage)
+    for shift, send in enumerate(sends, 1):
+        send[...] = jnp.where(partner(place, shift, stage[1]) > place, tail, head)
+
+
+def first_join_kernel(axes, count, last_stage, own_ref, *refs):
     groups = refs[:count]
-    own_out, group_out, weight_ref = refs[count:]
+    own_out, weight_ref, *group_outs = refs[count:]
     width = own_ref.shape[1] - LANES
     half = width + LANES // 2
     weights, lowest, highest = weigh(axes, own_ref, groups)
     store_weights(weight_ref, weights)
     own_out[:axes, :], own_out[axes:, :] = join_own(axes, own_ref, groups, weights)
-    group_out[:axes, :], group_out[axes:, :] = join_group(axes, groups, weights)
     mark(own_out, axes, own_ref[axes - 1 : axes, width : width + 1], own_ref[axes - 1 : axes, half : half + 1])
-    mark(group_out, axes, lowest, highest)
-
-
-def join_kernel(axes, count, own_ref, weight_ref, *refs):
+    head, tail = join_group(axes, groups, weights)
+    if last_stage is None:
+        group_outs[0][:axes, :] = head
+        group_outs[0][axes:, :] = tail
+    else:
+        put_sends(group_outs, last_stage, head, tail)
+    for out in group_outs:
+        mark(out, axes, lowest, highest)
+
+
+def join_kernel(axes, count, last_stage, own_ref, weight_ref, *refs):
     groups = refs[:count]
-    own_out, group_out = refs[count:]
+    own_out, *group_outs = refs[count:]
     weights = load_weights(weight_ref, count)
     own_out[:axes, :], own_out[axes:, :] = join_own(axes, own_ref, groups, weights)
-    group_out[:axes, :], group_out[axes:, :] = join_group(axes, groups, weights)
+    head, tail = join_group(axes, groups, weights)
+    if last_stage is None:
+        group_outs[0][:axes, :] = head
+        group_outs[0][axes:, :] = tail
+    else:
+        put_sends(group_outs, last_stage, head, tail)
+
+
+def weigh_last(axes, own, parts):
+    width = own.shape[1] - LANES
+    half = width + LANES // 2
+    first = own[axes - 1 : axes, width : width + 1]
+    last = own[axes - 1 : axes, half : half + 1]
+    weights = []
+    for part in parts:
+        head = part[axes - 1 : axes, width : width + 1]
+        tail = part[axes - 1 : axes, half : half + 1]
+        weights.append(
+            (
+                jnp.maximum(same(head, first), same(tail, first)),
+                jnp.maximum(same(head, last), same(tail, last)),
+            )
+        )
+    return weights
+
+
+def join_last(axes, own, parts, weights):
+    head, tail = own[:axes, :], own[axes:, :]
+    for part, (to_head, to_tail) in zip(parts, weights):
+        value = part[...]
+        head = head + to_head * value
+        tail = tail + to_tail * value
+    return head, tail
 
 
 def find_frames(axes, columns, centre, live, flat_ref, offset_ref):
@@ -244,10 +299,13 @@
     offset = offset_ref[:, :1]
     moment = jnp.zeros((SLOTS * axes, width), F32)
     columns = jnp.zeros((SLOTS * axes, LANES), F32)
+    spread = dot_nt(frames, points_ref[:BLOCK, :])
     for start in range(0, rows, BLOCK):
         block = points_ref[start : start + BLOCK, :]
         slot_of = nodes_ref[:, start : start + BLOCK] - first
-        terms = dot_nt(frames, block) - offset
+        terms = spread - offset
+        if start + BLOCK < rows:
+            spread = dot_nt(frames, points_ref[start + BLOCK : start + 2 * BLOCK, :])
         kept = [
             jnp.where(slot_of == slot, terms[slot * axes : (slot + 1) * axes], 0.0)
             for slot in range(SLOTS)
@@ -265,7 +323,7 @@
     for start in range(0, rows, BLOCK):
         block = points_ref[start : start + BLOCK, :]
         slot_of = nodes_ref[:, start : start + BLOCK] - first
-        terms = dot_nt(frames, block) - offset
+        terms = dot_nt(block, frames).T - offset
         out_ref[:, start : start + BLOCK] = sum(
             jnp.where(slot_of == slot, terms[slot * axes : (slot + 1) * axes], 0.0)
             for slot in range(SLOTS)
@@ -291,9 +349,9 @@
     width = points_ref.shape[1]
     first, last = ends_of(nodes_ref)
     span = last - first
-    weights, _, _ = weigh(axes, own_ref, groups)
+    weights = weigh_last(axes, own_ref, groups)
     store_weights(weight_ref, weights)
-    head, tail = join_own(axes, own_ref, groups, weights)
+    head, tail = join_last(axes, own_ref, groups, weights)
     flat = SLOTS * axes
     put_rows(whole_ref, part_ref[...], 0, flat)
     put_rows(whole_ref, tail[:, :width], pl.multiple_of(span * axes, axes), flat)
@@ -321,8 +379,8 @@
 def settle_frames(axes, nodes_ref, part_ref, centre_ref, own_ref, weight_ref, groups, flat_ref, offset_ref, whole_ref):
     first, last = ends_of(nodes_ref)
     span = last - first
-    weights = load_weights(weight_ref, len(groups))
-    head, tail = join_own(axes, own_ref, groups, weights)
+    weights = load_weights(weight_ref, len(groups), 2)
+    head, tail = join_last(axes, own_ref, groups, weights)
     flat = SLOTS * axes
     put_rows(whole_ref, part_ref[...], 0, flat)
     put_rows(whole_ref, tail, pl.multiple_of(span * axes, axes), flat)
@@ -353,15 +411,12 @@
 
 def radices(size):
     found = []
-    while size % 4 == 0:
-        found.append(4)
-        size //= 4
-    factor = 2
+    factor = 4
     while size > 1:
         while size % factor == 0:
-            found.insert(0, factor)
+            found.append(factor)
             size //= factor
-        factor += 1
+        factor = 2 if factor == 4 else factor + 1
     return found
 
 
@@ -375,18 +430,16 @@
     return stages
 
 
-def swap(value, stage, devices):
+def swap(values, stage, devices):
     stride, radix = stage
-    groups = [value]
-    for shift in range(1, radix):
+    received = []
+    for shift, value in enumerate(values, 1):
         pairs = []
         for source in range(devices):
             place = source // stride % radix
-            other = place ^ shift if radix & (radix - 1) == 0 else (place + shift) % radix
-            target = source + (other - place) * stride
-            pairs.append((source, target))
-        groups.append(lax.ppermute(value, ("row", "col"), pairs))
-    return groups
+            pairs.append((source, source + (partner(place, shift, radix) - place) * stride))
+        received.append(lax.ppermute(value, ("row", "col"), pairs))
+    return received
 
 
 def shape(*dims):
@@ -434,17 +487,20 @@
             limit=32,
             source=pltpu.HBM,
         )(*[pltpu.with_memory_space_constraint(each, pltpu.HBM) for each in (points, node_of_row.reshape(1, rows), init_axes.T)])
-        own = group = note
+        own = note
+        sends = [note]
         kept = []
-        for stage in stages[:-1]:
-            groups = swap(group, stage, devices)
+        for index, stage in enumerate(stages[:-1]):
+            groups = [sends[0]] + swap(sends * (stage[1] - 1), stage, devices)
             count = len(groups)
-            own, group, weight = call(
-                functools.partial(first_join_kernel, axes, count),
-                (shape(2 * axes, wide), shape(2 * axes, wide), shape(8 * count, LANES)),
+            ending = stages[-1] if index == len(stages) - 2 else None
+            outs = [shape(2 * axes, wide)] if ending is None else [shape(axes, wide)] * (ending[1] - 1)
+            own, weight, *sends = call(
+                functools.partial(first_join_kernel, axes, count, ending),
+                (shape(2 * axes, wide), shape(8 * count, LANES), *outs),
             )(own, *groups)
             kept.append(weight)
-        groups = swap(group, stages[-1], devices)
+        groups = swap(sends, stages[-1], devices)[::-1]
         count = len(groups)
         part, note, centre, weight = call(
             functools.partial(second_sweep_kernel, axes, count),
@@ -454,14 +510,17 @@
         )(points, nodes, init, part, sums, own, *groups)
         kept.append(weight)
         for repeat in range(1, ITERS):
-            own = group = note
-            for stage, weight in zip(stages[:-1], kept):
-                groups = swap(group, stage, devices)
-                own, group = call(
-                    functools.partial(join_kernel, axes, len(groups)),
-                    (shape(2 * axes, width), shape(2 * axes, width)),
-                )(own, weight, *groups)
-            groups = swap(group, stages[-1], devices)
+            own = note
+            sends = [note]
+            for index, stage in enumerate(stages[:-1]):
+                groups = [sends[0]] + swap(sends * (stage[1] - 1), stage, devices)
+                ending = stages[-1] if index == len(stages) - 2 else None
+                outs = [shape(2 * axes, width)] if ending is None else [shape(axes, width)] * (ending[1] - 1)
+                own, *sends = call(
+                    functools.partial(join_kernel, axes, len(groups), ending),
+                    (shape(2 * axes, width), *outs),
+                )(own, kept[index], *groups)
+            groups = swap(sends, stages[-1], devices)[::-1]
             settle = frame_scratch + [pltpu.VMEM((tall, LANES), F32)]
             if repeat < ITERS - 1:
                 part, note = call(

time: 80.6 us -> 76.3 us (0.947)
  waiting for transfers between devices: 26.8 us -> 23.5 us
  Pallas kernels: 27.8 us -> 26.9 us
    ppermute x21, waiting for transfers between devices: 26.8 us -> 23.5 us  [swap(): received.append(lax.ppermute(value, ('row', 'col'), pairs))]
    pallas_call x10, Pallas kernels: 27.8 us -> 26.9 us  [run(): pl.pallas_call(kernel, out_shape=outs, in_specs=[pl.BlockSpec(memory_spac...]
  transfers between devices with their start and end apart: 21 -> 21, of which waited for: 15 -> 18; matrix products, arithmetic and copies ran while one was open for 0% -> 0% of each run, Pallas kernels for 0% -> 0%
where the time goes in v3:
time: 76.3 us; the launch traced here: 76.2 us
  Pallas kernels  26.9 us (35%)
  starting transfers between devices  25.7 us (34%)
  waiting for transfers between devices  23.5 us (31%)
    pallas_call x10, Pallas kernels, run(): pl.pallas_call(kernel, out_shape=outs, in_specs=[pl.BlockSpec(memory_spac...  26.9 us
    ppermute x21, starting transfers between devices, swap(): received.append(lax.ppermute(value, ('row', 'col'), pairs))  25.7 us
    ppermute x21, waiting for transfers between devices, swap(): received.append(lax.ppermute(value, ('row', 'col'), pairs))  23.5 us
  transfers between devices with their start and end apart: 21, of which 18 were waited for; matrix products, arithmetic and copies ran while one was open for 0% of the time, Pallas kernels for 0%

profile of v3, /device:TPU:0, one launch (start us, length us, event | category | flops | bytes accessed | tf_op | source)
XLA Modules:
  0.0 76.2 jit_solution(15497292660476270540)
XLA Ops:
  0.0 7.7 %shard_map.37 = (f32[64,768]{1,0:T(8,128)S(1)}, f32[8,896]{1,0:T(8,128)S(1)}, f32[16,896]{1,0:T(8,128)S(1)}, bf16[8192,768]{1,0:T(8,128)(2,1)S(1)}, s32[1,8192]{1,0:T(1,128)S(1)}, /*index=5*/f32[8,768]{1,0:T(8,128)S(1)}) custom-call(bf16[8192,768]{1,0:T(8,128)(2,1)} %points_hbm.1, s32[1,8192]{1,0:T(1,128)} %bitcast.2, f32[8,768]{1,0:T(8,128)} %bitcast.3), custom_call_target="tpu_custom_call" | custom-call | tf_op jit(solution)/shard_map/pallas_call | solution.py:453
  7.7 4.0 %collective-permute-start.2 = (f32[16,896]{1,0:T(8,128)S(1)}, f32[16,896]{1,0:T(8,128)S(1)}, u32[]{:S(2)}, u32[]{:S(2)}) collective-permute-start(f32[16,896]{1,0:T(8,128)S(1)} %get-tuple-element.42.own_ref.refs_0_), channel_id=1, source_target_pairs={{0,3},{1,2},{2,1},{3,0},{4,7},{5,6},{6,5},{7,4},{8,11},{9,10},{10,... | collective-permute-start | bytes 172040 | tf_op jit(solution)/shard_map/ppermute | solution.py:441
  11.7 0.5 collective-permute-start.1
  12.2 0.2 collective-permute-start
  12.4 1.6 %collective-permute-done.2.refs_3_ = f32[16,896]{1,0:T(8,128)S(1)} collective-permute-done((f32[16,896]{1,0:T(8,128)S(1)}, f32[16,896]{1,0:T(8,128)S(1)}, u32[]{:S(2)}, u32[]{:S(2)}) %collective-permute-start.2) | collective-permute-done | bytes 57376 | tf_op jit(solution)/shard_map/ppermute | solution.py:441
  14.0 1.9 %collective-permute-done.1.refs_2_ = f32[16,896]{1,0:T(8,128)S(1)} collective-permute-done((f32[16,896]{1,0:T(8,128)S(1)}, f32[16,896]{1,0:T(8,128)S(1)}, u32[]{:S(2)}, u32[]{:S(2)}) %collective-permute-start.1) | collective-permute-done | bytes 57376 | tf_op jit(solution)/shard_map/ppermute | solution.py:441
  15.9 0.5 collective-permute-done.refs_1_
  16.4 0.3 shard_map.38
  16.6 2.7 %collective-permute-start.3 = (f32[16,896]{1,0:T(8,128)S(1)}, f32[16,896]{1,0:T(8,128)S(1)}, u32[]{:S(2)}, u32[]{:S(2)}) collective-permute-start(f32[16,896]{1,0:T(8,128)S(1)} %get-tuple-element.44.refs_0_), channel_id=1, source_target_pairs={{0,4},{1,5},{2,6},{3,7},{4,0},{5,1},{6,2},{7,3},{8,12},{9,13},{10,... | collective-permute-start | bytes 172040 | tf_op jit(solution)/shard_map/ppermute | solution.py:441
  19.3 2.5 %collective-permute-done.3.refs_1_ = f32[16,896]{1,0:T(8,128)S(1)} collective-permute-done((f32[16,896]{1,0:T(8,128)S(1)}, f32[16,896]{1,0:T(8,128)S(1)}, u32[]{:S(2)}, u32[]{:S(2)}) %collective-permute-start.3) | collective-permute-done | bytes 57376 | tf_op jit(solution)/shard_map/ppermute | solution.py:441
  21.8 0.2 shard_map.39
  22.0 0.1 collective-permute-start.4
  22.1 1.6 %collective-permute-start.5 = (f32[8,896]{1,0:T(8,128)S(1)}, f32[8,896]{1,0:T(8,128)S(1)}, u32[]{:S(2)}, u32[]{:S(2)}) collective-permute-start(f32[8,896]{1,0:T(8,128)S(1)} %get-tuple-element.47), channel_id=1, source_target_pairs={{0,16},{1,17},{2,18},{3,19},{4,20},{5,21},{6,22},{7,23},{8,24},{9,... | collective-permute-start | bytes 86024 | tf_op jit(solution)/shard_map/ppermute | solution.py:441
  23.7 0.3 collective-permute-start.6
  23.9 1.7 %collective-permute-done.4.refs_0_ = f32[8,896]{1,0:T(8,128)S(1)} collective-permute-done((f32[8,896]{1,0:T(8,128)S(1)}, f32[8,896]{1,0:T(8,128)S(1)}, u32[]{:S(2)}, u32[]{:S(2)}) %collective-permute-start.4) | collective-permute-done | bytes 28704 | tf_op jit(solution)/shard_map/ppermute | solution.py:441
  25.6 0.4 collective-permute-done.5.refs_1_
  26.0 6.6 %shard_map.40 = (f32[64,768]{1,0:T(8,128)S(1)}, f32[16,768]{1,0:T(8,128)S(1)}, f32[8,768]{1,0:T(8,128)S(1)}, f32[24,128]{1,0:T(8,128)S(1)}) custom-call(bf16[8192,768]{1,0:T(8,128)(2,1)S(1)} %get-tuple-element.37.points_ref, s32[1,8192]{1,0:T(1,128)S(1)} %get-tuple-element.38.nodes_ref, f32[8,768]{1,0:T(8,128)S(1)} %get-tuple-element.39.init_ref, ...), custom_call_target="tpu_custom_call" | custom-call | tf_op jit(solution)/shard_map/pallas_call | solution.py:453
  32.6 1.6 %collective-permute-start.9 = (f32[16,768]{1,0:T(8,128)S(1)}, f32[16,768]{1,0:T(8,128)S(1)}, u32[]{:S(2)}, u32[]{:S(2)}) collective-permute-start(f32[16,768]{1,0:T(8,128)S(1)} %get-tuple-element.51.own_ref.refs_0_), channel_id=1, source_target_pairs={{0,3},{1,2},{2,1},{3,0},{4,7},{5,6},{6,5},{7,4},{8,11},{9,10},{10,... | collective-permute-start | bytes 147464 | tf_op jit(solution)/shard_map/ppermute | solution.py:441
  34.2 0.3 collective-permute-start.8
  34.5 1.7 %collective-permute-start.7 = (f32[16,768]{1,0:T(8,128)S(1)}, f32[16,768]{1,0:T(8,128)S(1)}, u32[]{:S(2)}, u32[]{:S(2)}) collective-permute-start(f32[16,768]{1,0:T(8,128)S(1)} %get-tuple-element.51.own_ref.refs_0_), channel_id=1, source_target_pairs={{0,1},{1,0},{2,3},{3,2},{4,5},{5,4},{6,7},{7,6},{8,9},{9,8},{10,11... | collective-permute-start | bytes 147464 | tf_op jit(solution)/shard_map/ppermute | solution.py:441
  36.2 1.6 %collective-permute-done.9.refs_3_ = f32[16,768]{1,0:T(8,128)S(1)} collective-permute-done((f32[16,768]{1,0:T(8,128)S(1)}, f32[16,768]{1,0:T(8,128)S(1)}, u32[]{:S(2)}, u32[]{:S(2)}) %collective-permute-start.9) | collective-permute-done | bytes 49184 | tf_op jit(solution)/shard_map/ppermute | solution.py:441
  37.8 0.5 collective-permute-done.8.refs_2_
  38.3 0.4 collective-permute-done.7.refs_1_
  38.7 0.1 shard_map.41
  38.8 2.9 %collective-permute-start.10 = (f32[16,768]{1,0:T(8,128)S(1)}, f32[16,768]{1,0:T(8,128)S(1)}, u32[]{:S(2)}, u32[]{:S(2)}) collective-permute-start(f32[16,768]{1,0:T(8,128)S(1)} %get-tuple-element.55.refs_0_), channel_id=1, source_target_pairs={{0,4},{1,5},{2,6},{3,7},{4,0},{5,1},{6,2},{7,3},{8,12},{9,13},{10,... | collective-permute-start | bytes 147464 | tf_op jit(solution)/shard_map/ppermute | solution.py:441
  41.7 2.7 %collective-permute-done.10.refs_1_ = f32[16,768]{1,0:T(8,128)S(1)} collective-permute-done((f32[16,768]{1,0:T(8,128)S(1)}, f32[16,768]{1,0:T(8,128)S(1)}, u32[]{:S(2)}, u32[]{:S(2)}) %collective-permute-start.10) | collective-permute-done | bytes 49184 | tf_op jit(solution)/shard_map/ppermute | solution.py:441
  44.4 0.1 shard_map.42
  44.4 0.1 collective-permute-start.11
  44.5 1.1 %collective-permute-start.12 = (f32[8,768]{1,0:T(8,128)S(1)}, f32[8,768]{1,0:T(8,128)S(1)}, u32[]{:S(2)}, u32[]{:S(2)}) collective-permute-start(f32[8,768]{1,0:T(8,128)S(1)} %get-tuple-element.59), channel_id=1, source_target_pairs={{0,16},{1,17},{2,18},{3,19},{4,20},{5,21},{6,22},{7,23},{8,24},{9,... | collective-permute-start | bytes 73736 | tf_op jit(solution)/shard_map/ppermute | solution.py:441
  45.6 0.7 collective-permute-start.13
  46.4 1.4 %collective-permute-done.11.refs_0_ = f32[8,768]{1,0:T(8,128)S(1)} collective-permute-done((f32[8,768]{1,0:T(8,128)S(1)}, f32[8,768]{1,0:T(8,128)S(1)}, u32[]{:S(2)}, u32[]{:S(2)}) %collective-permute-start.11) | collective-permute-done | bytes 24608 | tf_op jit(solution)/shard_map/ppermute | solution.py:441
  47.7 0.8 %collective-permute-done.12.refs_1_ = f32[8,768]{1,0:T(8,128)S(1)} collective-permute-done((f32[8,768]{1,0:T(8,128)S(1)}, f32[8,768]{1,0:T(8,128)S(1)}, u32[]{:S(2)}, u32[]{:S(2)}) %collective-permute-start.12) | collective-permute-done | bytes 24608 | tf_op jit(solution)/shard_map/ppermute | solution.py:441
  48.5 6.7 %shard_map.43 = (f32[64,768]{1,0:T(8,128)S(1)}, f32[16,768]{1,0:T(8,128)S(1)}) custom-call(bf16[8192,768]{1,0:T(8,128)(2,1)S(1)} %get-tuple-element.37.points_ref, s32[1,8192]{1,0:T(1,128)S(1)} %get-tuple-element.38.nodes_ref, f32[64,768]{1,0:T(8,128)S(1)} %get-tuple-element.49.part_ref, f32[8,768]{1,0:T(8,128)S(1)} %get-tuple-element.50.centre_ref, ...), custom_call_target="tpu_custom_call" | custom-call | tf_op jit(solution)/shard_map/pallas_call | solution.py:453
  55.2 2.1 %collective-permute-start.16 = (f32[16,768]{1,0:T(8,128)S(1)}, f32[16,768]{1,0:T(8,128)S(1)}, u32[]{:S(2)}, u32[]{:S(2)}) collective-permute-start(f32[16,768]{1,0:T(8,128)S(1)} %get-tuple-element.62.own_ref.refs_0_), channel_id=1, source_target_pairs={{0,3},{1,2},{2,1},{3,0},{4,7},{5,6},{6,5},{7,4},{8,11},{9,10},{10,... | collective-permute-start | bytes 147464 | tf_op jit(solution)/shard_map/ppermute | solution.py:441
  57.3 0.3 collective-permute-start.15
  57.7 1.1 %collective-permute-start.14 = (f32[16,768]{1,0:T(8,128)S(1)}, f32[16,768]{1,0:T(8,128)S(1)}, u32[]{:S(2)}, u32[]{:S(2)}) collective-permute-start(f32[16,768]{1,0:T(8,128)S(1)} %get-tuple-element.62.own_ref.refs_0_), channel_id=1, source_target_pairs={{0,1},{1,0},{2,3},{3,2},{4,5},{5,4},{6,7},{7,6},{8,9},{9,8},{10,11... | collective-permute-start | bytes 147464 | tf_op jit(solution)/shard_map/ppermute | solution.py:441
  58.8 1.7 %collective-permute-done.16.refs_3_ = f32[16,768]{1,0:T(8,128)S(1)} collective-permute-done((f32[16,768]{1,0:T(8,128)S(1)}, f32[16,768]{1,0:T(8,128)S(1)}, u32[]{:S(2)}, u32[]{:S(2)}) %collective-permute-start.16) | collective-permute-done | bytes 49184 | tf_op jit(solution)/shard_map/ppermute | solution.py:441
  60.5 1.0 %collective-permute-done.15.refs_2_ = f32[16,768]{1,0:T(8,128)S(1)} collective-permute-done((f32[16,768]{1,0:T(8,128)S(1)}, f32[16,768]{1,0:T(8,128)S(1)}, u32[]{:S(2)}, u32[]{:S(2)}) %collective-permute-start.15) | collective-permute-done | bytes 49184 | tf_op jit(solution)/shard_map/ppermute | solution.py:441
  61.4 0.3 collective-permute-done.14.refs_1_
  61.8 0.1 shard_map.44
  61.9 2.6 %collective-permute-start.17 = (f32[16,768]{1,0:T(8,128)S(1)}, f32[16,768]{1,0:T(8,128)S(1)}, u32[]{:S(2)}, u32[]{:S(2)}) collective-permute-start(f32[16,768]{1,0:T(8,128)S(1)} %get-tuple-element.64.refs_0_), channel_id=1, source_target_pairs={{0,4},{1,5},{2,6},{3,7},{4,0},{5,1},{6,2},{7,3},{8,12},{9,13},{10,... | collective-permute-start | bytes 147464 | tf_op jit(solution)/shard_map/ppermute | solution.py:441
  64.5 2.4 %collective-permute-done.17.refs_1_ = f32[16,768]{1,0:T(8,128)S(1)} collective-permute-done((f32[16,768]{1,0:T(8,128)S(1)}, f32[16,768]{1,0:T(8,128)S(1)}, u32[]{:S(2)}, u32[]{:S(2)}) %collective-permute-start.17) | collective-permute-done | bytes 49184 | tf_op jit(solution)/shard_map/ppermute | solution.py:441
  67.0 0.1 collective-permute-start.18
  67.1 1.5 %collective-permute-start.19 = (f32[8,768]{1,0:T(8,128)S(1)}, f32[8,768]{1,0:T(8,128)S(1)}, u32[]{:S(2)}, u32[]{:S(2)}) collective-permute-start(f32[8,768]{1,0:T(8,128)S(1)} %get-tuple-element.67), channel_id=1, source_target_pairs={{0,16},{1,17},{2,18},{3,19},{4,20},{5,21},{6,22},{7,23},{8,24},{9,... | collective-permute-start | bytes 73736 | tf_op jit(solution)/shard_map/ppermute | solution.py:441
  68.6 0.3 collective-permute-start.20
  68.9 1.6 %collective-permute-done.18.refs_0_ = f32[8,768]{1,0:T(8,128)S(1)} collective-permute-done((f32[8,768]{1,0:T(8,128)S(1)}, f32[8,768]{1,0:T(8,128)S(1)}, u32[]{:S(2)}, u32[]{:S(2)}) %collective-permute-start.18) | collective-permute-done | bytes 24608 | tf_op jit(solution)/shard_map/ppermute | solution.py:441
  70.6 0.4 collective-permute-done.19.refs_1_
  71.0 5.2 %shard_map.46 = f32[8,8192]{1,0:T(8,128)} custom-call(bf16[8192,768]{1,0:T(8,128)(2,1)S(1)} %get-tuple-element.37.points_ref, s32[1,8192]{1,0:T(1,128)S(1)} %get-tuple-element.38.nodes_ref, f32[64,768]{1,0:T(8,128)S(1)} %get-tuple-element.61.part_ref, f32[8,768]{1,0:T(8,128)S(1)} %get-tuple-element.50.centre_ref, f32[16,768]{1,0:T(8,128)S(1)} %get-tuple-element.65.own_ref, ...), custom_call_target="tpu_custom_call" | custom-call | tf_op jit(solution)/shard_map/pallas_call | solution.py:453
  (4 shorter events, 0.1 us)
Async XLA Ops:
  7.7 6.3 %collective-permute-start.2 = (f32[16,896]{1,0:T(8,128)S(1)}, f32[16,896]{1,0:T(8,128)S(1)}, u32[]{:S(2)}, u32[]{:S(2)}) collective-permute-start(f32[16,896]{1,0:T(8,128)S(1)} %get-tuple-element.42.own_ref.refs_0_), channel_id=1, source_target_pairs={{0,3},{1,2},{2,1},{3,0},{4,7},{5,6},{6,5},{7,4},{8,11},{9,10},{10,... | collective-permute-start | bytes 172040 | tf_op jit(solution)/shard_map/ppermute | solution.py:441
  11.7 4.2 %collective-permute-start.1 = (f32[16,896]{1,0:T(8,128)S(1)}, f32[16,896]{1,0:T(8,128)S(1)}, u32[]{:S(2)}, u32[]{:S(2)}) collective-permute-start(f32[16,896]{1,0:T(8,128)S(1)} %get-tuple-element.42.own_ref.refs_0_), channel_id=1, source_target_pairs={{0,2},{1,3},{2,0},{3,1},{4,6},{5,7},{6,4},{7,5},{8,10},{9,11},{10,... | collective-permute-start | bytes 172040 | tf_op jit(solution)/shard_map/ppermute | solution.py:441
  12.2 4.2 %collective-permute-start = (f32[16,896]{1,0:T(8,128)S(1)}, f32[16,896]{1,0:T(8,128)S(1)}, u32[]{:S(2)}, u32[]{:S(2)}) collective-permute-start(f32[16,896]{1,0:T(8,128)S(1)} %get-tuple-element.42.own_ref.refs_0_), channel_id=1, source_target_pairs={{0,1},{1,0},{2,3},{3,2},{4,5},{5,4},{6,7},{7,6},{8,9},{9,8},{10,11... | collective-permute-start | bytes 172040 | tf_op jit(solution)/shard_map/ppermute | solution.py:441
  16.6 5.1 %collective-permute-start.3 = (f32[16,896]{1,0:T(8,128)S(1)}, f32[16,896]{1,0:T(8,128)S(1)}, u32[]{:S(2)}, u32[]{:S(2)}) collective-permute-start(f32[16,896]{1,0:T(8,128)S(1)} %get-tuple-element.44.refs_0_), channel_id=1, source_target_pairs={{0,4},{1,5},{2,6},{3,7},{4,0},{5,1},{6,2},{7,3},{8,12},{9,13},{10,... | collective-permute-start | bytes 172040 | tf_op jit(solution)/shard_map/ppermute | solution.py:441
  22.0 3.6 %collective-permute-start.4 = (f32[8,896]{1,0:T(8,128)S(1)}, f32[8,896]{1,0:T(8,128)S(1)}, u32[]{:S(2)}, u32[]{:S(2)}) collective-permute-start(f32[8,896]{1,0:T(8,128)S(1)} %get-tuple-element.46), channel_id=1, source_target_pairs={{0,24},{1,25},{2,26},{3,27},{4,28},{5,29},{6,30},{7,31},{8,16},{9,... | collective-permute-start | bytes 86024 | tf_op jit(solution)/shard_map/ppermute | solution.py:441
  22.1 3.9 %collective-permute-start.5 = (f32[8,896]{1,0:T(8,128)S(1)}, f32[8,896]{1,0:T(8,128)S(1)}, u32[]{:S(2)}, u32[]{:S(2)}) collective-permute-start(f32[8,896]{1,0:T(8,128)S(1)} %get-tuple-element.47), channel_id=1, source_target_pairs={{0,16},{1,17},{2,18},{3,19},{4,20},{5,21},{6,22},{7,23},{8,24},{9,... | collective-permute-start | bytes 86024 | tf_op jit(solution)/shard_map/ppermute | solution.py:441
  23.7 2.3 %collective-permute-start.6 = (f32[8,896]{1,0:T(8,128)S(1)}, f32[8,896]{1,0:T(8,128)S(1)}, u32[]{:S(2)}, u32[]{:S(2)}) collective-permute-start(f32[8,896]{1,0:T(8,128)S(1)} %get-tuple-element.48), channel_id=1, source_target_pairs={{0,8},{1,9},{2,10},{3,11},{4,12},{5,13},{6,14},{7,15},{8,0},{9,1},... | collective-permute-start | bytes 86024 | tf_op jit(solution)/shard_map/ppermute | solution.py:441
  32.6 5.2 %collective-permute-start.9 = (f32[16,768]{1,0:T(8,128)S(1)}, f32[16,768]{1,0:T(8,128)S(1)}, u32[]{:S(2)}, u32[]{:S(2)}) collective-permute-start(f32[16,768]{1,0:T(8,128)S(1)} %get-tuple-element.51.own_ref.refs_0_), channel_id=1, source_target_pairs={{0,3},{1,2},{2,1},{3,0},{4,7},{5,6},{6,5},{7,4},{8,11},{9,10},{10,... | collective-permute-start | bytes 147464 | tf_op jit(solution)/shard_map/ppermute | solution.py:441
  34.2 4.1 %collective-permute-start.8 = (f32[16,768]{1,0:T(8,128)S(1)}, f32[16,768]{1,0:T(8,128)S(1)}, u32[]{:S(2)}, u32[]{:S(2)}) collective-permute-start(f32[16,768]{1,0:T(8,128)S(1)} %get-tuple-element.51.own_ref.refs_0_), channel_id=1, source_target_pairs={{0,2},{1,3},{2,0},{3,1},{4,6},{5,7},{6,4},{7,5},{8,10},{9,11},{10,... | collective-permute-start | bytes 147464 | tf_op jit(solution)/shard_map/ppermute | solution.py:441
  34.5 4.2 %collective-permute-start.7 = (f32[16,768]{1,0:T(8,128)S(1)}, f32[16,768]{1,0:T(8,128)S(1)}, u32[]{:S(2)}, u32[]{:S(2)}) collective-permute-start(f32[16,768]{1,0:T(8,128)S(1)} %get-tuple-element.51.own_ref.refs_0_), channel_id=1, source_target_pairs={{0,1},{1,0},{2,3},{3,2},{4,5},{5,4},{6,7},{7,6},{8,9},{9,8},{10,11... | collective-permute-start | bytes 147464 | tf_op jit(solution)/shard_map/ppermute | solution.py:441
  38.8 5.6 %collective-permute-start.10 = (f32[16,768]{1,0:T(8,128)S(1)}, f32[16,768]{1,0:T(8,128)S(1)}, u32[]{:S(2)}, u32[]{:S(2)}) collective-permute-start(f32[16,768]{1,0:T(8,128)S(1)} %get-tuple-element.55.refs_0_), channel_id=1, source_target_pairs={{0,4},{1,5},{2,6},{3,7},{4,0},{5,1},{6,2},{7,3},{8,12},{9,13},{10,... | collective-permute-start | bytes 147464 | tf_op jit(solution)/shard_map/ppermute | solution.py:441
  44.4 3.3 %collective-permute-start.11 = (f32[8,768]{1,0:T(8,128)S(1)}, f32[8,768]{1,0:T(8,128)S(1)}, u32[]{:S(2)}, u32[]{:S(2)}) collective-permute-start(f32[8,768]{1,0:T(8,128)S(1)} %get-tuple-element.58), channel_id=1, source_target_pairs={{0,24},{1,25},{2,26},{3,27},{4,28},{5,29},{6,30},{7,31},{8,16},{9,... | collective-permute-start | bytes 73736 | tf_op jit(solution)/shard_map/ppermute | solution.py:441
  44.5 4.0 %collective-permute-start.12 = (f32[8,768]{1,0:T(8,128)S(1)}, f32[8,768]{1,0:T(8,128)S(1)}, u32[]{:S(2)}, u32[]{:S(2)}) collective-permute-start(f32[8,768]{1,0:T(8,128)S(1)} %get-tuple-element.59), channel_id=1, source_target_pairs={{0,16},{1,17},{2,18},{3,19},{4,20},{5,21},{6,22},{7,23},{8,24},{9,... | collective-permute-start | bytes 73736 | tf_op jit(solution)/shard_map/ppermute | solution.py:441
  45.6 2.9 %collective-permute-start.13 = (f32[8,768]{1,0:T(8,128)S(1)}, f32[8,768]{1,0:T(8,128)S(1)}, u32[]{:S(2)}, u32[]{:S(2)}) collective-permute-start(f32[8,768]{1,0:T(8,128)S(1)} %get-tuple-element.60), channel_id=1, source_target_pairs={{0,8},{1,9},{2,10},{3,11},{4,12},{5,13},{6,14},{7,15},{8,0},{9,1},... | collective-permute-start | bytes 73736 | tf_op jit(solution)/shard_map/ppermute | solution.py:441
  55.2 5.3 %collective-permute-start.16 = (f32[16,768]{1,0:T(8,128)S(1)}, f32[16,768]{1,0:T(8,128)S(1)}, u32[]{:S(2)}, u32[]{:S(2)}) collective-permute-start(f32[16,768]{1,0:T(8,128)S(1)} %get-tuple-element.62.own_ref.refs_0_), channel_id=1, source_target_pairs={{0,3},{1,2},{2,1},{3,0},{4,7},{5,6},{6,5},{7,4},{8,11},{9,10},{10,... | collective-permute-start | bytes 147464 | tf_op jit(solution)/shard_map/ppermute | solution.py:441
  57.3 4.1 %collective-permute-start.15 = (f32[16,768]{1,0:T(8,128)S(1)}, f32[16,768]{1,0:T(8,128)S(1)}, u32[]{:S(2)}, u32[]{:S(2)}) collective-permute-start(f32[16,768]{1,0:T(8,128)S(1)} %get-tuple-element.62.own_ref.refs_0_), channel_id=1, source_target_pairs={{0,2},{1,3},{2,0},{3,1},{4,6},{5,7},{6,4},{7,5},{8,10},{9,11},{10,... | collective-permute-start | bytes 147464 | tf_op jit(solution)/shard_map/ppermute | solution.py:441
  57.7 4.1 %collective-permute-start.14 = (f32[16,768]{1,0:T(8,128)S(1)}, f32[16,768]{1,0:T(8,128)S(1)}, u32[]{:S(2)}, u32[]{:S(2)}) collective-permute-start(f32[16,768]{1,0:T(8,128)S(1)} %get-tuple-element.62.own_ref.refs_0_), channel_id=1, source_target_pairs={{0,1},{1,0},{2,3},{3,2},{4,5},{5,4},{6,7},{7,6},{8,9},{9,8},{10,11... | collective-permute-start | bytes 147464 | tf_op jit(solution)/shard_map/ppermute | solution.py:441
  61.9 5.1 %collective-permute-start.17 = (f32[16,768]{1,0:T(8,128)S(1)}, f32[16,768]{1,0:T(8,128)S(1)}, u32[]{:S(2)}, u32[]{:S(2)}) collective-permute-start(f32[16,768]{1,0:T(8,128)S(1)} %get-tuple-element.64.refs_0_), channel_id=1, source_target_pairs={{0,4},{1,5},{2,6},{3,7},{4,0},{5,1},{6,2},{7,3},{8,12},{9,13},{10,... | collective-permute-start | bytes 147464 | tf_op jit(solution)/shard_map/ppermute | solution.py:441
  67.0 3.6 %collective-permute-start.18 = (f32[8,768]{1,0:T(8,128)S(1)}, f32[8,768]{1,0:T(8,128)S(1)}, u32[]{:S(2)}, u32[]{:S(2)}) collective-permute-start(f32[8,768]{1,0:T(8,128)S(1)} %get-tuple-element.66), channel_id=1, source_target_pairs={{0,24},{1,25},{2,26},{3,27},{4,28},{5,29},{6,30},{7,31},{8,16},{9,... | collective-permute-start | bytes 73736 | tf_op jit(solution)/shard_map/ppermute | solution.py:441
  67.1 3.9 %collective-permute-start.19 = (f32[8,768]{1,0:T(8,128)S(1)}, f32[8,768]{1,0:T(8,128)S(1)}, u32[]{:S(2)}, u32[]{:S(2)}) collective-permute-start(f32[8,768]{1,0:T(8,128)S(1)} %get-tuple-element.67), channel_id=1, source_target_pairs={{0,16},{1,17},{2,18},{3,19},{4,20},{5,21},{6,22},{7,23},{8,24},{9,... | collective-permute-start | bytes 73736 | tf_op jit(solution)/shard_map/ppermute | solution.py:441
  68.6 2.4 %collective-permute-start.20 = (f32[8,768]{1,0:T(8,128)S(1)}, f32[8,768]{1,0:T(8,128)S(1)}, u32[]{:S(2)}, u32[]{:S(2)}) collective-permute-start(f32[8,768]{1,0:T(8,128)S(1)} %get-tuple-element.68), channel_id=1, source_target_pairs={{0,8},{1,9},{2,10},{3,11},{4,12},{5,13},{6,14},{7,15},{8,0},{9,1},... | collective-permute-start | bytes 73736 | tf_op jit(solution)/shard_map/ppermute | solution.py:441
